TPU v7x, 256 devices: a whole 4x4x8 slice. The times are simulated.
256 devices in a mesh: pool: 2 (over core), ep: 128 (over x, z, y).
Axes of the slice: x: 4, y: 4, z: 8, core: 2. Of those that a mesh axis runs over, the one named last changes fastest.
Arguments:
- queries: bfloat16 [1024, 147456], P(('pool', 'ep')), may hold values from -90 to 90
- new_latent: bfloat16 [1024, 1152], P(('pool', 'ep')), may hold values from -6 to 6
- resident_cache: bfloat16 [768, 294912], P(('pool', 'ep')), may hold values from -6 to 6
- resident_len: int32 [768], P(('pool', 'ep')), may hold values from 1 to 512, as said below
- fresh_cache: bfloat16 [256, 294912], P(('pool', 'ep')), may hold values from -6 to 6
- fresh_len: int32 [2, 128], replicated, may hold values from 1 to 512, as said below
- matching: int32 [2, 128], replicated, may hold values from 0 to 127, each once within a row
Outputs:
- context: bfloat16 [1024, 131072], P(('pool', 'ep'))
Inputs may be any that keep to these rules, and one draw needn't show every extreme that they name: `matching`: each row is a permutation. `resident_len`: some request has 512 positions. `fresh_len`: some request has 512 positions.
All inputs are finite; a program needn't handle non-finite values.
Results may differ from a plain program's by a relative error of at most 0.0048.
Values may be sent and summed in bfloat16 or wider, within the bound.
No kernel may reach another device: no remote copies, remote signals or barrier semaphores. Data moves between devices by JAX's collectives and lax.ppermute only.
A program may use at most 64 MiB of HBM per device.

v0:
```python
import jax
import jax.numpy as jnp
from jax import lax
from jax.sharding import PartitionSpec as P

LAT = 512
STEPS = 2


score_scale = 192.0 ** (-0.5)


def swapped(block, axis, distance):
    count = lax.axis_size(axis)
    route = []
    for low in range(count):
        high = low | 1 << distance
        if high != low and high < count:
            route += [(low, high), (high, low)]
    return lax.ppermute(block, axis, route)


def attend(queries, caches, lengths, latents, lat_width):
    old_scores = (
        jnp.einsum("rthk,rck->rthc", queries, caches, preferred_element_type=jnp.float32)
        * score_scale
    )
    new_scores = (
        jnp.einsum("rthk,rsk->rths", queries, latents, preferred_element_type=jnp.float32)
        * score_scale
    )
    positions = jnp.arange(caches.shape[1], dtype=jnp.int32)
    live_old = (positions[None, :] < lengths[:, None])[:, None, None, :]
    step_order = jnp.arange(queries.shape[1], dtype=jnp.int32)
    live_new = (step_order[None, :] <= step_order[:, None])[None, :, None, :]
    old_scores = jnp.where(live_old, old_scores, -jnp.inf)
    new_scores = jnp.where(live_new, new_scores, -jnp.inf)
    peak_score = jnp.maximum(
        jnp.max(old_scores, axis=3, keepdims=True), jnp.max(new_scores, axis=3, keepdims=True)
    )
    old_exp = jnp.exp(old_scores - peak_score)
    new_exp = jnp.exp(new_scores - peak_score)
    denominator = jnp.sum(old_exp, axis=3, keepdims=True) + jnp.sum(new_exp, axis=3, keepdims=True)
    old_probs = (old_exp / denominator).astype(jnp.bfloat16)
    new_probs = (new_exp / denominator).astype(jnp.bfloat16)
    context = jnp.einsum(
        "rthc,rcl->rthl", old_probs, caches[:, :, :lat_width], preferred_element_type=jnp.float32
    )
    context = context + jnp.einsum(
        "rths,rsl->rthl", new_probs, latents[:, :, :lat_width], preferred_element_type=jnp.float32
    )
    return context.astype(jnp.bfloat16)


def pull_request(payload, own_sources):
    partner_data = swapped(payload, "pool", 0)
    spread = lax.all_to_all(partner_data, "ep", split_axis=0, concat_axis=0, tiled=True)
    chosen = jnp.take(spread, own_sources, axis=0)
    return lax.all_to_all(chosen, "ep", split_axis=0, concat_axis=0, tiled=True)


def per_device(queries, new_latent, resident_cache, resident_len, fresh_cache, fresh_len, matching):
    row_count = queries.shape[0]
    res_count = resident_cache.shape[0]
    group_count = lax.axis_size("ep")
    pool_index = lax.axis_index("pool")
    ep_index = lax.axis_index("ep")
    step_count = STEPS
    kv_width = new_latent.shape[1] // step_count
    head_count = queries.shape[1] // (step_count * kv_width)
    cache_span = resident_cache.shape[1] // kv_width
    own_sources = matching[pool_index]
    query_grid = queries.reshape(row_count, step_count, head_count, kv_width)
    latent_grid = new_latent.reshape(row_count, step_count, kv_width)
    resident = resident_cache.reshape(res_count, cache_span, kv_width)
    arrived = pull_request(fresh_cache.reshape(group_count, -1), own_sources).reshape(
        1, cache_span, kv_width
    )
    arrive_len = fresh_len[1 - pool_index, own_sources[ep_index]]
    caches = jnp.concatenate([resident, arrived], axis=0)
    lengths = jnp.concatenate([resident_len, arrive_len[None]])
    context = attend(query_grid, caches, lengths, latent_grid, LAT)
    return context.reshape(row_count, -1)


def solution(mesh):
    return jax.shard_map(
        per_device,
        mesh=mesh,
        in_specs=(
            P(("pool", "ep"), None),
            P(("pool", "ep"), None),
            P(("pool", "ep"), None),
            P(("pool", "ep")),
            P(("pool", "ep"), None),
            P(),
            P(),
        ),
        out_specs=P(("pool", "ep"), None),
        check_vma=False,
    )
```

profile of v0, /device:TPU:32, one launch (start us, length us, event | category | flops | bytes accessed | tf_op | source)
XLA Modules:
  0.0 97.8 jit_solution(5839351076323616888)
XLA Ops:
  0.0 13.2 %reduce = bf16[294912]{0:T(1024)(128)(2,1)S(1)} reduce(bf16[1,294912]{1,0:T(2,128)(2,1)} %param.11, bf16[]{:T(256)} %constant.56), dimensions={0}, to_apply=%param.11.reduce_sub_computation | reduce | bytes 1179650 | tf_op args[4]
  13.2 0.7 reshape.124
  14.0 2.0 %collective-permute-done = bf16[128,2304]{1,0:T(8,128)(2,1)S(1)} collective-permute-done((bf16[128,2304]{1,0:T(8,128)(2,1)S(1)}, bf16[128,2304]{1,0:T(8,128)(2,1)S(1)}, u32[]{:S(2)}, u32[]{:S(2)}) %collective-permute-start) | collective-permute-done | bytes 589856 | tf_op jit(solution)/shard_map/ppermute | solution.py:20
  16.6 1.1 %reduce.2 = bf16[128,2304]{1,0:T(8,128)(2,1)S(1)} reduce(bf16[128,1,2304]{2,0,1:T(8,128)(2,1)S(1)} %bitcast.53, bf16[]{:T(256)} %broadcast.71), dimensions={1}, to_apply=%copy.25.reduce_sub_computation | reduce | bytes 1179650 | tf_op jit(solution)/shard_map/all_to_all | solution.py:57
  17.7 0.9 reshape.148
  18.6 15.0 %all-to-all-start = ((bf16[128,2,1152]{2,1,0:T(2,128)(2,1)}), bf16[128,2,1152]{2,1,0:T(2,128)(2,1)S(1)}, u32[]{:S(2)}, u32[]{:S(2)}) async-start(bf16[128,2,1152]{2,1,0:T(2,128)(2,1)} %reshape.148), calls=%async_computation | async-start | bytes 1179648 | tf_op jit(solution)/shard_map/all_to_all | solution.py:57
  33.7 20.8 %all-to-all-done = bf16[128,2,1152]{2,1,0:T(2,128)(2,1)S(1)} async-done(((bf16[128,2,1152]{2,1,0:T(2,128)(2,1)}), bf16[128,2,1152]{2,1,0:T(2,128)(2,1)S(1)}, u32[]{:S(2)}, u32[]{:S(2)}) %all-to-all-start) | async-done | bytes 589856 | tf_op jit(solution)/shard_map/all_to_all | solution.py:57
  55.1 1.0 gather_fusion
  56.2 1.2 %reduce.3 = bf16[128,2304]{1,0:T(8,128)(2,1)S(1)} reduce(bf16[128,1,2304]{2,0,1:T(8,128)(2,1)S(1)} %bitcast_select_fusion, bf16[]{:T(256)} %broadcast.71), dimensions={1}, to_apply=%copy.26.reduce_sub_computation | reduce | bytes 1179650 | tf_op jit(solution)/shard_map/jit(_take)/select_n | solution.py:58
  57.4 0.9 reshape.150
  58.4 7.2 %all-to-all-start.1 = ((bf16[128,2,1152]{2,1,0:T(2,128)(2,1)}), bf16[128,2,1152]{2,1,0:T(2,128)(2,1)S(1)}, u32[]{:S(2)}, u32[]{:S(2)}) async-start(bf16[128,2,1152]{2,1,0:T(2,128)(2,1)} %reshape.150), calls=%async_computation.1 | async-start | bytes 1179648 | tf_op jit(solution)/shard_map/all_to_all | solution.py:59
  67.7 3.5 %reshape.144 = bf16[884736]{0:T(1024)(128)(2,1)} reshape(bf16[3,294912]{1,0:T(4,128)(2,1)S(1)} %copy-done) | data formatting | bytes 3538944
  71.2 3.3 %reshape.123 = bf16[3,512,576]{2,1,0:T(8,128)(2,1)S(1)} reshape(bf16[884736]{0:T(1024)(128)(2,1)} %reshape.144) | data formatting | bytes 3538944 | tf_op jit(solution)/shard_map/reshape | solution.py:75
  74.5 2.2 %copy.27 = bf16[3,512,576]{1,2,0:T(8,128)(2,1)} copy(bf16[3,512,576]{2,1,0:T(8,128)(2,1)S(1)} %reshape.123) | data formatting | bytes 3538944 | tf_op jit(solution)/shard_map/reshape | solution.py:75
  76.7 2.5 %reshape.146 = bf16[589824]{0:T(1024)(128)(2,1)S(1)} reshape(bf16[4,147456]{1,0:T(4,128)(2,1)} %param.7) | data formatting | bytes 2359296
  79.2 1.1 %reshape.126 = bf16[4,2,128,576]{3,2,1,0:T(8,128)(2,1)S(1)} reshape(bf16[589824]{0:T(1024)(128)(2,1)S(1)} %reshape.146) | data formatting | bytes 2359296 | tf_op jit(solution)/shard_map/reshape | solution.py:73
  81.6 0.7 pad_add_fusion
  82.9 2.3 %all-to-all-done.1 = bf16[128,2,1152]{2,1,0:T(2,128)(2,1)S(1)} async-done(((bf16[128,2,1152]{2,1,0:T(2,128)(2,1)}), bf16[128,2,1152]{2,1,0:T(2,128)(2,1)S(1)}, u32[]{:S(2)}, u32[]{:S(2)}) %all-to-all-start.1) | async-done | bytes 589856 | tf_op jit(solution)/shard_map/all_to_all | solution.py:59
  85.6 3.6 %reduce.1 = bf16[128,2304]{1,0:T(8,128)(2,1)S(1)} reduce(bf16[128,1,2304]{2,1,0:T(2,128)(2,1)S(1)} %reshape.151, bf16[]{:T(256)} %constant.56), dimensions={1}, to_apply=%all_to_all.15.reduce_sub_computation | reduce | bytes 1179650 | tf_op jit(solution)/shard_map/all_to_all | solution.py:59
  89.2 0.7 reshape.125
  90.2 2.6 %bitcast_reduce_fusion = (f32[4,2,128]{2,1,0:T(2,128)S(1)}, f32[4,512,2,128]{3,1,2,0:T(8,128)S(1)}) fusion(pred[4,512]{1,0:T(4,128)(4,1)S(1)} %iota_compare_fusion, bf16[4,2,128,576]{3,2,1,0:T(8,128)(2,1)S(1)} %reshape.126, bf16[1,512,576]{1,2,0:T(8,128)(2,1)S(1)} %copy.28, bf16[3,512,576]{1,2,0:T(8,128)(2,1)} %copy.27), kind=kOutput, calls=%fused_computation.10 | convolution fusion | flops 610270208 | bytes 5642240 | tf_op jit(solution)/shard_map/rthk,rck->rthc/dot_general | solution.py:25
  93.5 0.8 copy-done.1
  94.3 1.2 %fusion.5 = f32[4,2,128,512]{3,2,1,0:T(8,128)S(1)} fusion(bf16[3,512,576]{1,2,0:T(8,128)(2,1)S(1)} %copy-done.1, bf16[1,512,576]{1,2,0:T(8,128)(2,1)S(1)} %copy.28, f32[4,512,2,128]{3,1,2,0:T(8,128)S(1)} %get-tuple-element.6, f32[4,2,128]{2,1,0:T(2,128)S(1)} %add.55, f32[4,2,128]{2,1,0:T(2,128)S(1)} %max.8, pred[4,512]{1,0:T(4,128)(4,1)S(1)} %iota_compare_fusion), kind=kOutput, calls=%fused_computation.8 | convolution fusion | flops 540540928 | bytes 6563840 | tf_op jit(solution)/shard_map/rthc,rcl->rthl/dot_general | solution.py:46
  96.0 1.8 %copy.43 = bf16[1,4,256,512]{3,1,2,0:T(4,128)(2,1)} copy(bf16[1,4,256,512]{3,2,1,0:T(8,128)(2,1)S(1)} %bitcast.52) | data formatting | bytes 2097152
  (33 shorter events, 5.3 us)
Async XLA Ops:
  13.2 20.4 %copy-start.3 = (s32[2,128]{1,0:T(2,128)S(1)}, s32[2,128]{1,0:T(2,128)}, u32[]{:S(2)}) copy-start(s32[2,128]{1,0:T(2,128)} %param.13) | copy-start | bytes 3076
  13.9 2.1 %collective-permute-start = (bf16[128,2304]{1,0:T(8,128)(2,1)S(1)}, bf16[128,2304]{1,0:T(8,128)(2,1)S(1)}, u32[]{:S(2)}, u32[]{:S(2)}) collective-permute-start(bf16[128,2304]{1,0:T(8,128)(2,1)S(1)} %reshape.124), channel_id=1, source_target_pairs={{0,128},{128,0},{1,129},{129,1},{2,130},{130,2},{3,131},{131,3},{4... | collective-permute-start | bytes 1769480 | tf_op jit(solution)/shard_map/ppermute | solution.py:20
  18.6 35.8 %all-to-all-start = ((bf16[128,2,1152]{2,1,0:T(2,128)(2,1)}), bf16[128,2,1152]{2,1,0:T(2,128)(2,1)S(1)}, u32[]{:S(2)}, u32[]{:S(2)}) async-start(bf16[128,2,1152]{2,1,0:T(2,128)(2,1)} %reshape.148), calls=%async_computation | async-start | bytes 1179648 | tf_op jit(solution)/shard_map/all_to_all | solution.py:57
  56.0 11.4 %copy-start.2 = (bf16[4,1152]{1,0:T(4,128)(2,1)S(1)}, bf16[4,1152]{1,0:T(4,128)(2,1)}, u32[]{:S(2)}) copy-start(bf16[4,1152]{1,0:T(4,128)(2,1)} %param.8) | copy-start | bytes 27652
  56.2 11.5 %copy-start = (bf16[3,294912]{1,0:T(4,128)(2,1)S(1)}, bf16[3,294912]{1,0:T(4,128)(2,1)}, u32[]{:S(2)}) copy-start(bf16[3,294912]{1,0:T(4,128)(2,1)} %param.9) | copy-start | bytes 5308420
  58.4 26.7 %all-to-all-start.1 = ((bf16[128,2,1152]{2,1,0:T(2,128)(2,1)}), bf16[128,2,1152]{2,1,0:T(2,128)(2,1)S(1)}, u32[]{:S(2)}, u32[]{:S(2)}) async-start(bf16[128,2,1152]{2,1,0:T(2,128)(2,1)} %reshape.150), calls=%async_computation.1 | async-start | bytes 1179648 | tf_op jit(solution)/shard_map/all_to_all | solution.py:59
  76.7 4.2 %copy-start.4 = (s32[2,128]{1,0:T(2,128)S(1)}, s32[2,128]{1,0:T(2,128)}, u32[]{:S(2)}) copy-start(s32[2,128]{1,0:T(2,128)} %param.12) | copy-start | bytes 3076
  76.7 4.9 %copy-start.5 = (s32[3]{0:T(128)S(1)}, s32[3]{0:T(128)}, u32[]{:S(2)}) copy-start(s32[3]{0:T(128)} %param.10) | copy-start | bytes 40
  92.8 1.5 %copy-start.1 = (bf16[3,512,576]{1,2,0:T(8,128)(2,1)S(1)}, bf16[3,512,576]{1,2,0:T(8,128)(2,1)}, u32[]{:S(2)}) copy-start(bf16[3,512,576]{1,2,0:T(8,128)(2,1)} %copy.27) | copy-start | bytes 5308420
where the time goes:
time: 98.2 us; the launch traced here: 97.8 us
  waiting for transfers between devices  25 us (25%)
  local copies, waits for them, and re-layouts  22.8 us (23%)
  starting transfers between devices  22.3 us (23%)
  other arithmetic  20.7 us (21%)
  matrix products  4.82 us (5%)
  between operations  2.18 us (2%)
    all_to_all x1, waiting for transfers between devices, pull_request(): lax.all_to_all(partner_data, 'ep', split_axis=0, concat_axis=0, tiled=True)  20.8 us
    all_to_all x1, starting transfers between devices, pull_request(): lax.all_to_all(partner_data, 'ep', split_axis=0, concat_axis=0, tiled=True)  15 us
    unnamed x1, other arithmetic  13.2 us
    unnamed x20, local copies, waits for them, and re-layouts  11.5 us
    all_to_all x1, starting transfers between devices, pull_request(): return lax.all_to_all(chosen, 'ep', split_axis=0, concat_axis=0, tiled=True)  7.16 us
    reshape x2, local copies, waits for them, and re-layouts, per_device(): resident = resident_cache.reshape(res_count, cache_span, kv_width)  5.52 us
    all_to_all x1, other arithmetic, pull_request(): return lax.all_to_all(chosen, 'ep', split_axis=0, concat_axis=0, tiled=True)  3.56 us
    dot_general x1, matrix products, attend(): jnp.einsum('rthk,rck->rthc', queries, caches, preferred_element_type=jnp....  2.64 us
  transfers between devices with their start and end apart: 3, of which 3 were waited for; matrix products, arithmetic and copies ran while one was open for 16% of the time, Pallas kernels for 0%

commit v1 on v0

v1 whole, which is shorter than its diff:
```python
import jax
import jax.numpy as jnp
from jax import lax
from jax.experimental import pallas as pl
from jax.experimental.pallas import tpu as pltpu
from jax.sharding import PartitionSpec as P

LAT = 512
KV = 576
STEPS = 2
HEADS = 128
CTX = 512
LANES = 128
PAIRS = CTX // 2
PAIR_ROWS = 2 * KV // LANES
CACHE_ROWS = CTX * KV // LANES
QUERY_ROWS = STEPS * HEADS * KV // LANES
BF, F32 = jnp.bfloat16, jnp.float32

score_scale = 192.0 ** (-0.5)
in_vmem = pl.BlockSpec(memory_space=pltpu.VMEM)
in_smem = pl.BlockSpec(memory_space=pltpu.SMEM)
params = pltpu.CompilerParams(vmem_limit_bytes=40 << 20)


def flat_row(src, row, flat, count):
    for at in range(0, count, LANES):
        piece = src[pl.ds(row, 1), pl.ds(at * LANES, LANES * LANES)]
        flat[pl.ds(at, LANES), :] = piece.astype(F32).reshape(LANES, LANES)


def halves(tiles):
    even = jnp.concatenate(tiles[:5], axis=1)[:, :KV]
    odd = jnp.concatenate(tiles[4:], axis=1)[:, KV - LAT : KV - LAT + KV]
    return even, odd


def strided_halves(flat, pairs):
    return halves([flat[pl.ds(j, pairs, PAIR_ROWS), :].astype(BF) for j in range(PAIR_ROWS)])


def padded_latents(new, row):
    lat = new[pl.ds(row, 1), :].astype(F32)
    rows = [lat[:, s * KV : (s + 1) * KV] for s in range(STEPS)]
    return jnp.concatenate(rows + [jnp.zeros((8 - STEPS, KV), F32)], axis=0).astype(BF)


def attend(queries, key_even, key_odd, length, latents):
    both_last = (((1,), (1,)), ((), ()))

    def scores(keys):
        return lax.dot_general(queries, keys, both_last, preferred_element_type=F32) * score_scale

    even, odd, new = scores(key_even), scores(key_odd), scores(latents)
    position = 2 * lax.broadcasted_iota(jnp.int32, even.shape, 1)
    even = jnp.where(position < length, even, -jnp.inf)
    odd = jnp.where(position + 1 < length, odd, -jnp.inf)
    row = lax.broadcasted_iota(jnp.int32, new.shape, 0)
    step = jnp.where((row & (HEADS - 1)) >= HEADS // 2, 1, 0)
    new = jnp.where(lax.broadcasted_iota(jnp.int32, new.shape, 1) <= step, new, -jnp.inf)
    parts = (even, odd, new)
    peak = jnp.max(even, axis=1, keepdims=True)
    for part in parts[1:]:
        peak = jnp.maximum(peak, jnp.max(part, axis=1, keepdims=True))
    exps = [jnp.exp(part - peak) for part in parts]
    inverse = 1.0 / sum(jnp.sum(e, axis=1, keepdims=True) for e in exps)
    context = 0.0
    for e, values in zip(exps, (key_even, key_odd, latents)):
        probs = (e * inverse).astype(BF)
        context = context + jnp.dot(probs, values[:, :LAT], preferred_element_type=F32)
    return context.astype(BF)


def fresh_kernel(src, out, flat):
    flat_row(src, 0, flat, CACHE_ROWS)
    for g in range(PAIRS // 16):
        for j in range(PAIR_ROWS):
            tile = flat[pl.ds(g * 16 * PAIR_ROWS + j, 16, PAIR_ROWS), :]
            out[pl.ds((g * PAIR_ROWS + j) * 16, 16), :] = tile.astype(BF)


def fresh_tiles(fresh):
    return pl.pallas_call(
        fresh_kernel,
        out_shape=jax.ShapeDtypeStruct((CACHE_ROWS, LANES), BF),
        in_specs=[in_vmem],
        out_specs=in_vmem,
        scratch_shapes=[pltpu.VMEM((CACHE_ROWS, LANES), F32)],
        compiler_params=params,
        name="fresh_tiles",
    )(fresh)


def gather_kernel(sources, blocks, out):
    def some(i, carry):
        for u in range(8):
            out[i * 8 + u] = blocks[sources[i * 8 + u]]
        return carry

    lax.fori_loop(0, out.shape[0] // 8, some, 0)


def gather_blocks(sources, blocks):
    return pl.pallas_call(
        gather_kernel,
        out_shape=jax.ShapeDtypeStruct(blocks.shape, BF),
        in_specs=[in_smem, in_vmem],
        out_specs=in_vmem,
        compiler_params=params,
        name="gather_blocks",
    )(sources, blocks)


def resident_kernel(lengths, queries, new, caches, context, last_queries, last_latents, query_flat, cache_flat):
    def queries_of(row):
        flat_row(queries, row, query_flat, QUERY_ROWS)
        return jnp.concatenate(strided_halves(query_flat, QUERY_ROWS // PAIR_ROWS), axis=0)

    count = caches.shape[0]
    for r in range(count):
        flat_row(caches, r, cache_flat, CACHE_ROWS)
        key_even, key_odd = strided_halves(cache_flat, PAIRS)
        context[r] = attend(queries_of(r), key_even, key_odd, lengths[r], padded_latents(new, r))
    last_queries[...] = queries_of(count)
    last_latents[...] = padded_latents(new, count)


def resident_attention(lengths, queries, new, caches):
    count = caches.shape[0]
    return pl.pallas_call(
        resident_kernel,
        out_shape=(
            jax.ShapeDtypeStruct((count, STEPS * HEADS, LAT), BF),
            jax.ShapeDtypeStruct((STEPS * HEADS, KV), BF),
            jax.ShapeDtypeStruct((8, KV), BF),
        ),
        in_specs=[in_smem, in_vmem, in_vmem, in_vmem],
        out_specs=(in_vmem, in_vmem, in_vmem),
        scratch_shapes=[pltpu.VMEM((QUERY_ROWS, LANES), F32), pltpu.VMEM((CACHE_ROWS, LANES), F32)],
        compiler_params=params,
        cost_estimate=pl.CostEstimate(flops=10**9, bytes_accessed=8 << 20, transcendentals=400000),
        name="resident_attention",
    )(lengths, queries, new, caches)


def arrived_kernel(length, queries, latents, keys, resident, out):
    tiles = keys[...].reshape(PAIRS // 16, PAIR_ROWS, 16, LANES)
    key_even, key_odd = halves([tiles[:, j].reshape(PAIRS, LANES) for j in range(PAIR_ROWS)])
    count = resident.shape[0]
    out[0:count] = resident[...]
    out[count] = attend(queries[...], key_even, key_odd, length[0], latents[...])


def arrived_attention(length, queries, latents, keys, resident):
    return pl.pallas_call(
        arrived_kernel,
        out_shape=jax.ShapeDtypeStruct((resident.shape[0] + 1,) + resident.shape[1:], BF),
        in_specs=[in_smem, in_vmem, in_vmem, in_vmem, in_vmem],
        out_specs=in_vmem,
        compiler_params=params,
        name="arrived_attention",
    )(length, queries, latents, keys, resident)


def per_device(queries, new_latent, resident_cache, resident_len, fresh_cache, fresh_len, matching):
    group_count = lax.axis_size("ep")
    pool_index = lax.axis_index("pool")
    own_sources = matching[pool_index]
    tiles = fresh_tiles(fresh_cache)
    tiles = lax.ppermute(tiles, "pool", [(0, 1), (1, 0)])
    blocks = tiles.reshape(group_count, PAIR_ROWS, 2, LANES)
    blocks = lax.all_to_all(blocks, "ep", split_axis=0, concat_axis=0, tiled=True)
    resident, last_queries, last_latents = resident_attention(resident_len, queries, new_latent, resident_cache)
    blocks, resident = lax.optimization_barrier((blocks, resident))
    blocks = gather_blocks(own_sources, blocks)
    blocks = lax.all_to_all(blocks, "ep", split_axis=0, concat_axis=0, tiled=True)
    arrive_len = fresh_len[1 - pool_index, own_sources[lax.axis_index("ep")]]
    context = arrived_attention(
        arrive_len[None], last_queries, last_latents, blocks.reshape(CACHE_ROWS, LANES), resident
    )
    rows = context.shape[0]
    context = context.reshape(rows, 2, STEPS * HEADS // 2, LAT).transpose(0, 2, 1, 3)
    return context.reshape(rows, -1)


def solution(mesh):
    return jax.shard_map(
        per_device,
        mesh=mesh,
        in_specs=(
            P(("pool", "ep"), None),
            P(("pool", "ep"), None),
            P(("pool", "ep"), None),
            P(("pool", "ep")),
            P(("pool", "ep"), None),
            P(),
            P(),
        ),
        out_specs=P(("pool", "ep"), None),
        check_vma=False,
    )
```

time: 98.2 us -> 72.9 us (0.74)
  other arithmetic: 20.7 us -> 0 us
  local copies, waits for them, and re-layouts: 22.8 us -> 6.91 us
  Pallas kernels: 0 us -> 9.9 us
  waiting for transfers between devices: 25 us -> 31.5 us
  matrix products: 4.82 us -> 0 us
    unnamed x1 -> x0, other arithmetic: 13.2 us -> none
    pallas_call x0 -> x4, Pallas kernels: none -> 9.9 us  [the longest x1 6.08 us: resident_attention(): pl.pallas_call(resident_kernel, out_shape=(jax.ShapeDtypeStruct((count, S...]
    unnamed x20 -> x14, local copies, waits for them, and re-layouts: 11.5 us -> 2.95 us
    reshape x8 -> x1, local copies, waits for them, and re-layouts: 8.46 us -> 1.64 us  [per_device(): return context.reshape(rows, -1)]
    all_to_all x2, waiting for transfers between devices: 23 us -> 29.4 us  [per_device(): lax.all_to_all(blocks, 'ep', split_axis=0, concat_axis=0, tiled=True)]
    dot_general x4 -> x0, matrix products: 4.82 us -> none  [the longest x1 2.64 us: attend(): jnp.einsum('rthk,rck->rthc', queries, caches, preferred_element_type=jnp....]
    all_to_all x2 -> x0, other arithmetic: 4.66 us -> none  [the longest x1 3.56 us: pull_request(): return lax.all_to_all(chosen, 'ep', split_axis=0, concat_axis=0, tiled=True)]
    select_n x3 -> x0, other arithmetic: 1.38 us -> none  [pull_request(): chosen = jnp.take(spread, own_sources, axis=0)]
  transfers between devices with their start and end apart: 3 -> 3, of which waited for: 3 -> 3; matrix products, arithmetic and copies ran while one was open for 16% -> 2% of each run, Pallas kernels for 0% -> 8%
where the time goes in v1:
time: 72.9 us; the launch traced here: 72.6 us
  waiting for transfers between devices  31.5 us (43%)
  starting transfers between devices  22.3 us (31%)
  Pallas kernels  9.9 us (14%)
  local copies, waits for them, and re-layouts  6.91 us (9%)
  between operations  2.03 us (3%)
    all_to_all x2, waiting for transfers between devices, per_device(): lax.all_to_all(blocks, 'ep', split_axis=0, concat_axis=0, tiled=True)  29.4 us
    all_to_all x2, starting transfers between devices, per_device(): lax.all_to_all(blocks, 'ep', split_axis=0, concat_axis=0, tiled=True)  22.2 us
    pallas_call x1, Pallas kernels, resident_attention(): pl.pallas_call(resident_kernel, out_shape=(jax.ShapeDtypeStruct((count, S...  6.08 us
    unnamed x14, local copies, waits for them, and re-layouts  2.95 us
    ppermute x1, waiting for transfers between devices, per_device(): tiles = lax.ppermute(tiles, 'pool', [(0, 1), (1, 0)])  2.12 us
    pallas_call x1, Pallas kernels, arrived_attention(): pl.pallas_call(arrived_kernel, out_shape=jax.ShapeDtypeStruct((resident.s...  1.96 us
    reshape x1, local copies, waits for them, and re-layouts, per_device(): return context.reshape(rows, -1)  1.64 us
    pallas_call x1, Pallas kernels, gather_blocks(): pl.pallas_call(gather_kernel, out_shape=jax.ShapeDtypeStruct(blocks.shape...  1.6 us
  transfers between devices with their start and end apart: 3, of which 3 were waited for; matrix products, arithmetic and copies ran while one was open for 2% of the time, Pallas kernels for 8%

profile of v1, /device:TPU:32, one launch (start us, length us, event | category | flops | bytes accessed | tf_op | source)
XLA Modules:
  0.0 72.6 jit_solution(15988530381764886246)
XLA Ops:
  0.0 0.0 copy-start
  0.0 1.3 %copy-done = bf16[1,294912]{1,0:T(2,128)(2,1)S(1)} copy-done((bf16[1,294912]{1,0:T(2,128)(2,1)S(1)}, bf16[1,294912]{1,0:T(2,128)(2,1)}, u32[]{:S(2)}) %copy-start) | copy-done | bytes 589848
  1.3 0.0 copy-start.2
  1.3 0.3 fresh_tiles.1
  1.5 0.1 collective-permute-start
  1.6 2.1 %collective-permute-done = bf16[2304,128]{1,0:T(8,128)(2,1)} collective-permute-done((bf16[2304,128]{1,0:T(8,128)(2,1)S(1)}, bf16[2304,128]{1,0:T(8,128)(2,1)}, u32[]{:S(2)}, u32[]{:S(2)}) %collective-permute-start) | collective-permute-done | bytes 589856 | tf_op jit(solution)/shard_map/ppermute | solution.py:170
  3.8 15.0 %all-to-all-start = ((bf16[128,9,2,128]{3,2,1,0:T(2,128)(2,1)}), bf16[128,9,2,128]{3,2,1,0:T(2,128)(2,1)S(1)}, u32[]{:S(2)}, u32[]{:S(2)}) async-start(bf16[128,9,2,128]{3,2,1,0:T(2,128)(2,1)} %bitcast.3), calls=%async_computation | async-start | bytes 1179648 | tf_op jit(solution)/shard_map/all_to_all | solution.py:172
  18.8 0.0 copy-done.2
  18.8 0.0 copy-done.3
  18.8 0.0 copy-done.4
  18.8 0.0 copy-start.1
  18.8 1.7 %copy-done.1 = bf16[3,294912]{1,0:T(4,128)(2,1)S(1)} copy-done((bf16[3,294912]{1,0:T(4,128)(2,1)S(1)}, bf16[3,294912]{1,0:T(4,128)(2,1)}, u32[]{:S(2)}) %copy-start.1) | copy-done | bytes 1769496
  20.5 6.1 %resident_attention.1 = (bf16[3,256,512]{2,1,0:T(8,128)(2,1)S(1)}, bf16[256,576]{1,0:T(8,128)(2,1)S(1)}, bf16[8,576]{1,0:T(8,128)(2,1)S(1)}) custom-call(s32[3]{0:T(128)S(1)} %copy-done.4, bf16[4,147456]{1,0:T(4,128)(2,1)S(1)} %copy-done.2, bf16[4,1152]{1,0:T(4,128)(2,1)S(1)} %copy-done.3, bf16[3,294912]{1,0:T(4,128)(2,1)S(1)} %copy-done.1), custom_call_target="tpu_custom_call" | custom-call | flops 1000000000 | bytes 8388608 | tf_op jit(solution)/shard_map/resident_attention/pallas_call | solution.py:130
  26.6 0.0 copy-done.5
  26.6 13.0 %all-to-all-done.blocks = bf16[128,9,2,128]{3,2,1,0:T(2,128)(2,1)S(1)} async-done(((bf16[128,9,2,128]{3,2,1,0:T(2,128)(2,1)}), bf16[128,9,2,128]{3,2,1,0:T(2,128)(2,1)S(1)}, u32[]{:S(2)}, u32[]{:S(2)}) %all-to-all-start) | async-done | bytes 589856 | tf_op jit(solution)/shard_map/all_to_all | solution.py:172
  39.6 1.6 %gather_blocks.1 = bf16[128,9,2,128]{3,2,1,0:T(2,128)(2,1)} custom-call(s32[128]{0:T(128)S(1)} %dynamic-slice_bitcast_fusion.sources, bf16[128,9,2,128]{3,2,1,0:T(2,128)(2,1)S(1)} %all-to-all-done.blocks), custom_call_target="tpu_custom_call" | custom-call | tf_op jit(solution)/shard_map/gather_blocks/pallas_call | solution.py:104
  41.2 7.2 %all-to-all-start.1 = ((bf16[128,9,2,128]{3,2,1,0:T(2,128)(2,1)}), bf16[128,9,2,128]{3,2,1,0:T(2,128)(2,1)S(1)}, u32[]{:S(2)}, u32[]{:S(2)}) async-start(bf16[128,9,2,128]{3,2,1,0:T(2,128)(2,1)} %gather_blocks.1), calls=%async_computation.1 | async-start | bytes 1179648 | tf_op jit(solution)/shard_map/all_to_all | solution.py:176
  48.4 0.6 dynamic_slice.9
  50.9 0.0 copy-done.6
  50.9 0.6 dynamic_slice.10
  51.5 16.4 %all-to-all-done.1 = bf16[128,9,2,128]{3,2,1,0:T(2,128)(2,1)S(1)} async-done(((bf16[128,9,2,128]{3,2,1,0:T(2,128)(2,1)}), bf16[128,9,2,128]{3,2,1,0:T(2,128)(2,1)S(1)}, u32[]{:S(2)}, u32[]{:S(2)}) %all-to-all-start.1) | async-done | bytes 589856 | tf_op jit(solution)/shard_map/all_to_all | solution.py:176
  67.9 2.0 %arrived_attention.1 = bf16[4,256,512]{2,1,0:T(8,128)(2,1)S(1)} custom-call(s32[1]{0:T(128)} %bitcast.1.length, bf16[256,576]{1,0:T(8,128)(2,1)S(1)} %get-tuple-element.10.queries, bf16[8,576]{1,0:T(8,128)(2,1)S(1)} %get-tuple-element.11.latents, bf16[2304,128]{1,0:T(8,128)(2,1)S(1)} %bitcast.10, bf16[3,256,512]{2,1,0:T(8,128)(2,1)S(1)} %get-tuple-element.14.resident), custom_call_target="tpu_custom_call" | custom-call | tf_op jit(solution)/shard_map/arrived_attention/pallas_call | solution.py:155
  69.9 1.1 %copy.8 = bf16[4,128,2,512]{3,2,1,0:T(2,128)(2,1)S(1)} copy(bf16[4,128,2,512]{3,1,2,0:T(8,128)(2,1)S(1)} %bitcast.9) | data formatting | bytes 2097152 | tf_op jit(solution)/shard_map/transpose | solution.py:182
  71.0 1.6 %reshape.17 = bf16[4,131072]{1,0:T(4,128)(2,1)} reshape(bf16[4,128,2,512]{3,2,1,0:T(2,128)(2,1)S(1)} %copy.8) | data formatting | bytes 2097152 | tf_op jit(solution)/shard_map/reshape | solution.py:183
  (5 shorter events, 0.0 us)
Async XLA Ops:
  0.0 1.3 %copy-start = (bf16[1,294912]{1,0:T(2,128)(2,1)S(1)}, bf16[1,294912]{1,0:T(2,128)(2,1)}, u32[]{:S(2)}) copy-start(bf16[1,294912]{1,0:T(2,128)(2,1)} %src.1) | copy-start | bytes 1769476
  1.3 17.5 %copy-start.2 = (bf16[4,147456]{1,0:T(4,128)(2,1)S(1)}, bf16[4,147456]{1,0:T(4,128)(2,1)}, u32[]{:S(2)}) copy-start(bf16[4,147456]{1,0:T(4,128)(2,1)} %queries.1) | copy-start | bytes 3538948
  1.3 17.5 %copy-start.3 = (bf16[4,1152]{1,0:T(4,128)(2,1)S(1)}, bf16[4,1152]{1,0:T(4,128)(2,1)}, u32[]{:S(2)}) copy-start(bf16[4,1152]{1,0:T(4,128)(2,1)} %new.1) | copy-start | bytes 27652
  1.3 17.5 %copy-start.4 = (s32[3]{0:T(128)S(1)}, s32[3]{0:T(128)}, u32[]{:S(2)}) copy-start(s32[3]{0:T(128)} %lengths.1) | copy-start | bytes 40
  1.5 2.2 %collective-permute-start = (bf16[2304,128]{1,0:T(8,128)(2,1)S(1)}, bf16[2304,128]{1,0:T(8,128)(2,1)}, u32[]{:S(2)}, u32[]{:S(2)}) collective-permute-start(bf16[2304,128]{1,0:T(8,128)(2,1)S(1)} %fresh_tiles.1), channel_id=1, source_target_pairs={{0,128},{128,0},{1,129},{129,1},{2,130},{130,2},{3,131},{131,3},{4... | collective-permute-start | bytes 1769480 | tf_op jit(solution)/shard_map/ppermute | solution.py:170
  3.8 35.8 %all-to-all-start = ((bf16[128,9,2,128]{3,2,1,0:T(2,128)(2,1)}), bf16[128,9,2,128]{3,2,1,0:T(2,128)(2,1)S(1)}, u32[]{:S(2)}, u32[]{:S(2)}) async-start(bf16[128,9,2,128]{3,2,1,0:T(2,128)(2,1)} %bitcast.3), calls=%async_computation | async-start | bytes 1179648 | tf_op jit(solution)/shard_map/all_to_all | solution.py:172
  18.8 1.7 %copy-start.1 = (bf16[3,294912]{1,0:T(4,128)(2,1)S(1)}, bf16[3,294912]{1,0:T(4,128)(2,1)}, u32[]{:S(2)}) copy-start(bf16[3,294912]{1,0:T(4,128)(2,1)} %caches.1) | copy-start | bytes 5308420
  20.5 6.1 %copy-start.5 = (s32[2,128]{1,0:T(2,128)S(1)}, s32[2,128]{1,0:T(2,128)}, u32[]{:S(2)}) copy-start(s32[2,128]{1,0:T(2,128)} %param.13) | copy-start | bytes 3076
  39.6 11.3 %copy-start.6 = (s32[2,128]{1,0:T(2,128)S(1)}, s32[2,128]{1,0:T(2,128)}, u32[]{:S(2)}) copy-start(s32[2,128]{1,0:T(2,128)} %param.12) | copy-start | bytes 3076
  41.2 26.7 %all-to-all-start.1 = ((bf16[128,9,2,128]{3,2,1,0:T(2,128)(2,1)}), bf16[128,9,2,128]{3,2,1,0:T(2,128)(2,1)S(1)}, u32[]{:S(2)}, u32[]{:S(2)}) async-start(bf16[128,9,2,128]{3,2,1,0:T(2,128)(2,1)} %gather_blocks.1), calls=%async_computation.1 | async-start | bytes 1179648 | tf_op jit(solution)/shard_map/all_to_all | solution.py:176

commit v2 on v1

v2 whole, which is shorter than its diff:
```python
import jax
import jax.numpy as jnp
from jax import lax
from jax.experimental import pallas as pl
from jax.experimental.pallas import tpu as pltpu
from jax.sharding import PartitionSpec as P

LAT = 512
KV = 576
STEPS = 2
HEADS = 128
CTX = 512
ROWS = 4
LANES = 128
PAIRS = CTX // 2
PAIR_ROWS = 2 * KV // LANES
CACHE_ROWS = CTX * KV // LANES
QUERY_ROWS = STEPS * HEADS * KV // LANES
CHUNKS = STEPS * HEADS * LAT // LANES
GATHER_PIECES = 4
BF, F32 = jnp.bfloat16, jnp.float32

score_scale = 192.0 ** (-0.5)
in_vmem = pl.BlockSpec(memory_space=pltpu.VMEM)
in_smem = pl.BlockSpec(memory_space=pltpu.SMEM)
small = pltpu.CompilerParams(vmem_limit_bytes=8 << 20)


def flat_row(src, row, flat, count):
    for at in range(0, count, LANES):
        piece = src[pl.ds(row, 1), pl.ds(at * LANES, LANES * LANES)]
        flat[pl.ds(at, LANES), :] = piece.astype(F32).reshape(LANES, LANES)


def halves(tiles):
    even = jnp.concatenate(tiles[:5], axis=1)[:, :KV]
    odd = jnp.concatenate(tiles[4:], axis=1)[:, KV - LAT : KV - LAT + KV]
    return even, odd


def strided_halves(flat, pairs):
    return halves([flat[pl.ds(j, pairs, PAIR_ROWS), :].astype(BF) for j in range(PAIR_ROWS)])


def padded_latents(new, row):
    lat = new[pl.ds(row, 1), :].astype(F32)
    rows = [lat[:, s * KV : (s + 1) * KV] for s in range(STEPS)]
    return jnp.concatenate(rows + [jnp.zeros((LANES - STEPS, KV), F32)], axis=0).astype(BF)


def by_step(even, odd):
    half = HEADS // 2
    return jnp.concatenate([x[s * half : (s + 1) * half] for s in range(STEPS) for x in (even, odd)], axis=0)


def probabilities(queries, keys, length):
    scores = lax.dot_general(queries, keys, (((1,), (1,)), ((), ())), preferred_element_type=F32) * score_scale
    column = lax.broadcasted_iota(jnp.int32, (1, CTX + LANES), 1)
    position = jnp.where(column < PAIRS, 2 * column, 2 * (column - PAIRS) + 1)
    step = lax.broadcasted_iota(jnp.int32, (STEPS * HEADS, 1), 0) >> (HEADS - 1).bit_length()
    live = jnp.where(column < CTX, position, column - CTX) < jnp.where(column < CTX, length, step + 1)
    scores = jnp.where(live, scores, -jnp.inf)
    exps = jnp.exp(scores - jnp.max(scores, axis=1, keepdims=True))
    return (exps * (1.0 / jnp.sum(exps, axis=1, keepdims=True))).astype(BF)


def put_context(rows, token, step, context):
    tokens = rows.shape[0] // CHUNKS
    half, chunks = HEADS // 2, LAT // LANES
    for parity in range(2):
        for k in range(chunks):
            at = (step * HEADS * chunks + parity * chunks + k) * tokens + token % tokens
            rows[pl.ds(at, half, 2 * chunks * tokens), :] = context[
                parity * half : (parity + 1) * half, k * LANES : (k + 1) * LANES
            ]


def fresh_kernel(src, out, flat):
    flat_row(src, 0, flat, CACHE_ROWS)
    for g in range(PAIRS // 16):
        for j in range(PAIR_ROWS):
            tile = flat[pl.ds(g * 16 * PAIR_ROWS + j, 16, PAIR_ROWS), :]
            out[pl.ds((g * PAIR_ROWS + j) * 16, 16), :] = tile.astype(BF)


def fresh_tiles(fresh):
    return pl.pallas_call(
        fresh_kernel,
        out_shape=jax.ShapeDtypeStruct((CACHE_ROWS, LANES), BF),
        in_specs=[in_vmem],
        out_specs=in_vmem,
        scratch_shapes=[pltpu.VMEM((CACHE_ROWS, LANES), F32)],
        compiler_params=small,
        name="fresh_tiles",
    )(fresh)


def gather_kernel(sources, blocks, out, picked, sems):
    size = out.shape[0] // GATHER_PIECES
    copies = []
    for piece in range(GATHER_PIECES):
        at = piece * size
        for d in range(at, at + size):
            picked[d] = blocks[sources[d]]
        copy = pltpu.make_async_copy(picked.at[pl.ds(at, size)], out.at[pl.ds(at, size)], sems.at[piece])
        copy.start()
        copies.append(copy)
    for copy in copies:
        copy.wait()


def gather_blocks(sources, blocks):
    return pl.pallas_call(
        gather_kernel,
        out_shape=jax.ShapeDtypeStruct(blocks.shape, BF),
        in_specs=[in_smem, in_vmem],
        out_specs=pl.BlockSpec(memory_space=pl.ANY),
        scratch_shapes=[pltpu.VMEM(blocks.shape, BF), pltpu.SemaphoreType.DMA((GATHER_PIECES,))],
        compiler_params=small,
        name="gather_blocks",
    )(sources, blocks)


def resident_kernel(
    lengths, queries, new, caches, out, third, last_queries, last_latents, query_flat, cache_flat, rows
):
    def queries_of(row):
        flat_row(queries, row, query_flat, QUERY_ROWS)
        return by_step(*strided_halves(query_flat, QUERY_ROWS // PAIR_ROWS))

    for r in range(ROWS - 1):
        flat_row(caches, r, cache_flat, CACHE_ROWS)
        keys = jnp.concatenate([*strided_halves(cache_flat, PAIRS), padded_latents(new, r)], axis=0)
        probs = probabilities(queries_of(r), keys, lengths[r])
        context = jnp.dot(probs, keys[:, :LAT], preferred_element_type=F32)
        for step in range(STEPS):
            put_context(rows, r, step, context[step * HEADS : (step + 1) * HEADS])
    for c in range(0, CHUNKS, LANES):
        piece = rows[pl.ds(c * ROWS, LANES * ROWS), :]
        out[pl.ds(c, LANES)] = piece.astype(BF).reshape(LANES, 2, 2, LANES)
    third[...] = rows[pl.ds(ROWS - 2, CHUNKS, ROWS), :]
    last_queries[...] = queries_of(ROWS - 1)
    last_latents[...] = padded_latents(new, ROWS - 1)


def resident_attention(lengths, queries, new, caches):
    return pl.pallas_call(
        resident_kernel,
        out_shape=(
            jax.ShapeDtypeStruct((CHUNKS, 2, 2, LANES), BF),
            jax.ShapeDtypeStruct((CHUNKS, LANES), F32),
            jax.ShapeDtypeStruct((STEPS * HEADS, KV), BF),
            jax.ShapeDtypeStruct((LANES, KV), BF),
        ),
        in_specs=[in_smem, in_vmem, in_vmem, in_vmem],
        out_specs=(in_vmem,) * 4,
        scratch_shapes=[
            pltpu.VMEM((QUERY_ROWS, LANES), F32),
            pltpu.VMEM((CACHE_ROWS, LANES), F32),
            pltpu.VMEM((ROWS * CHUNKS, LANES), F32),
        ],
        compiler_params=pltpu.CompilerParams(vmem_limit_bytes=32 << 20),
        cost_estimate=pl.CostEstimate(flops=10**9, bytes_accessed=8 << 20, transcendentals=400000),
        name="resident_attention",
    )(lengths, queries, new, caches)


def arrived_kernel(length, queries, latents, tiles, third, before, out, both, rows, sems):
    parts = tiles[...].reshape(PAIRS // 16, PAIR_ROWS, 16, LANES)
    halved = halves([parts[:, j].reshape(PAIRS, LANES) for j in range(PAIR_ROWS)])
    keys = jnp.concatenate([*halved, latents[...]], axis=0)
    both[pl.ds(0, CHUNKS, 2), :] = third[...]
    probs = probabilities(queries[...], keys, length[0])
    values = keys[:, :LAT]
    copies = []
    size = CHUNKS // STEPS
    for step in range(STEPS):
        context = jnp.dot(probs[step * HEADS : (step + 1) * HEADS], values, preferred_element_type=F32)
        put_context(both, ROWS - 1, step, context)
        place = pl.ds(step * size, size)
        for c in range(step * size, (step + 1) * size, LANES):
            rows[pl.ds(c, LANES)] = both[pl.ds(2 * c, 2 * LANES), :].astype(BF).reshape(LANES, 2, LANES)
        copy = pltpu.make_async_copy(rows.at[place], out.at[place, 1], sems.at[step])
        copy.start()
        copies.append(copy)
    for copy in copies:
        copy.wait()


def arrived_attention(length, queries, latents, tiles, third, before):
    whole = pl.BlockSpec(memory_space=pl.ANY)
    return pl.pallas_call(
        arrived_kernel,
        out_shape=jax.ShapeDtypeStruct(before.shape, BF),
        in_specs=[in_smem, in_vmem, in_vmem, in_vmem, in_vmem, whole],
        out_specs=whole,
        scratch_shapes=[
            pltpu.VMEM((2 * CHUNKS, LANES), F32),
            pltpu.VMEM((CHUNKS, 2, LANES), BF),
            pltpu.SemaphoreType.DMA((STEPS,)),
        ],
        input_output_aliases={5: 0},
        compiler_params=pltpu.CompilerParams(vmem_limit_bytes=24 << 20),
        name="arrived_attention",
    )(length, queries, latents, tiles, third, before)


def per_device(queries, new_latent, resident_cache, resident_len, fresh_cache, fresh_len, matching):
    group_count = lax.axis_size("ep")
    pool_index = lax.axis_index("pool")
    own_sources = matching[pool_index]
    tiles = fresh_tiles(fresh_cache)
    tiles = lax.ppermute(tiles, "pool", [(0, 1), (1, 0)])
    blocks = tiles.reshape(group_count, PAIR_ROWS, 2, LANES)
    blocks = lax.all_to_all(blocks, "ep", split_axis=0, concat_axis=0, tiled=True)
    out, third, last_queries, last_latents = resident_attention(resident_len, queries, new_latent, resident_cache)
    blocks, third = lax.optimization_barrier((blocks, third))
    blocks = gather_blocks(own_sources, blocks)
    blocks = lax.all_to_all(blocks, "ep", split_axis=0, concat_axis=0, tiled=True)
    arrive_len = fresh_len[1 - pool_index, own_sources[lax.axis_index("ep")]]
    tiles = blocks.reshape(CACHE_ROWS, LANES)
    out = arrived_attention(arrive_len[None], last_queries, last_latents, tiles, third, out)
    return out.transpose(1, 2, 0, 3).reshape(ROWS, -1)


def solution(mesh):
    return jax.shard_map(
        per_device,
        mesh=mesh,
        in_specs=(
            P(("pool", "ep"), None),
            P(("pool", "ep"), None),
            P(("pool", "ep"), None),
            P(("pool", "ep")),
            P(("pool", "ep"), None),
            P(),
            P(),
        ),
        out_specs=P(("pool", "ep"), None),
        check_vma=False,
    )
```

time: 72.9 us -> 70.7 us (0.970)
  local copies, waits for them, and re-layouts: 6.91 us -> 4.08 us
  Pallas kernels: 9.9 us -> 12.3 us
  waiting for transfers between devices: 31.5 us -> 30 us
    pallas_call x2, Pallas kernels: 8.05 us -> 10.7 us  [the longest x1 8.01 us: resident_attention(): pl.pallas_call(resident_kernel, out_shape=(jax.ShapeDtypeStruct((CHUNKS,...]
    reshape x1 -> x0, local copies, waits for them, and re-layouts: 1.64 us -> none  [per_device(): return context.reshape(rows, -1)]
    all_to_all x2, waiting for transfers between devices: 29.4 us -> 27.9 us  [per_device(): lax.all_to_all(blocks, 'ep', split_axis=0, concat_axis=0, tiled=True)]
    transpose x1 -> x0, local copies, waits for them, and re-layouts: 1.08 us -> none  [per_device(): context.reshape(rows, 2, STEPS * HEADS // 2, LAT).transpose(0, 2, 1, 3)]
  transfers between devices with their start and end apart: 3 -> 3, of which waited for: 3 -> 3; matrix products, arithmetic and copies ran while one was open for 2% -> 2% of each run, Pallas kernels for 8% -> 11%
where the time goes in v2:
time: 70.7 us; the launch traced here: 70.4 us
  waiting for transfers between devices  30 us (42%)
  starting transfers between devices  22.3 us (32%)
  Pallas kernels  12.3 us (17%)
  local copies, waits for them, and re-layouts  4.08 us (6%)
  between operations  1.75 us (2%)
    all_to_all x2, waiting for transfers between devices, per_device(): lax.all_to_all(blocks, 'ep', split_axis=0, concat_axis=0, tiled=True)  27.9 us
    all_to_all x2, starting transfers between devices, per_device(): lax.all_to_all(blocks, 'ep', split_axis=0, concat_axis=0, tiled=True)  22.2 us
    pallas_call x1, Pallas kernels, resident_attention(): pl.pallas_call(resident_kernel, out_shape=(jax.ShapeDtypeStruct((CHUNKS,...  8.01 us
    unnamed x14, local copies, waits for them, and re-layouts  2.95 us
    pallas_call x1, Pallas kernels, arrived_attention(): pl.pallas_call(arrived_kernel, out_shape=jax.ShapeDtypeStruct(before.shap...  2.64 us
    ppermute x1, waiting for transfers between devices, per_device(): tiles = lax.ppermute(tiles, 'pool', [(0, 1), (1, 0)])  2.12 us
    pallas_call x1, Pallas kernels, gather_blocks(): pl.pallas_call(gather_kernel, out_shape=jax.ShapeDtypeStruct(blocks.shape...  1.43 us
  transfers between devices with their start and end apart: 3, of which 3 were waited for; matrix products, arithmetic and copies ran while one was open for 2% of the time, Pallas kernels for 11%

profile of v2, /device:TPU:32, one launch (start us, length us, event | category | flops | bytes accessed | tf_op | source)
XLA Modules:
  0.0 70.4 jit_solution(7103140761113682859)
XLA Ops:
  0.0 0.0 copy-start
  0.0 1.3 %copy-done = bf16[1,294912]{1,0:T(2,128)(2,1)S(1)} copy-done((bf16[1,294912]{1,0:T(2,128)(2,1)S(1)}, bf16[1,294912]{1,0:T(2,128)(2,1)}, u32[]{:S(2)}) %copy-start) | copy-done | bytes 589848
  1.3 0.0 copy-start.2
  1.3 0.0 copy-start.3
  1.3 0.0 copy-start.4
  1.3 0.3 fresh_tiles.1
  1.5 0.1 collective-permute-start
  1.6 2.1 %collective-permute-done = bf16[2304,128]{1,0:T(8,128)(2,1)} collective-permute-done((bf16[2304,128]{1,0:T(8,128)(2,1)S(1)}, bf16[2304,128]{1,0:T(8,128)(2,1)}, u32[]{:S(2)}, u32[]{:S(2)}) %collective-permute-start) | collective-permute-done | bytes 589856 | tf_op jit(solution)/shard_map/ppermute | solution.py:213
  3.8 15.0 %all-to-all-start = ((bf16[128,9,2,128]{3,2,1,0:T(2,128)(2,1)}), bf16[128,9,2,128]{3,2,1,0:T(2,128)(2,1)S(1)}, u32[]{:S(2)}, u32[]{:S(2)}) async-start(bf16[128,9,2,128]{3,2,1,0:T(2,128)(2,1)} %bitcast.3), calls=%async_computation | async-start | bytes 1179648 | tf_op jit(solution)/shard_map/all_to_all | solution.py:215
  18.8 0.0 copy-done.2
  18.8 0.0 copy-done.3
  18.8 0.0 copy-done.4
  18.8 0.0 copy-start.1
  18.8 1.7 %copy-done.1 = bf16[3,294912]{1,0:T(4,128)(2,1)S(1)} copy-done((bf16[3,294912]{1,0:T(4,128)(2,1)S(1)}, bf16[3,294912]{1,0:T(4,128)(2,1)}, u32[]{:S(2)}) %copy-start.1) | copy-done | bytes 1769496
  20.5 8.0 %resident_attention.1 = (bf16[1024,2,2,128]{3,2,1,0:T(2,128)(2,1)}, f32[1024,128]{1,0:T(8,128)S(1)}, bf16[256,576]{1,0:T(8,128)(2,1)S(1)}, bf16[128,576]{1,0:T(8,128)(2,1)S(1)}) custom-call(s32[3]{0:T(128)S(1)} %copy-done.4, bf16[4,147456]{1,0:T(4,128)(2,1)S(1)} %copy-done.2, bf16[4,1152]{1,0:T(4,128)(2,1)S(1)} %copy-done.3, bf16[3,294912]{1,0:T(4,128)(2,1)S(1)} %copy-done.1), custom_call_target="tpu_custom_call" | custom-call | flops 1000000000 | bytes 8388608 | tf_op jit(solution)/shard_map/resident_attention/pallas_call | solution.py:147
  28.5 0.0 copy-done.5
  28.5 11.1 %all-to-all-done.blocks = bf16[128,9,2,128]{3,2,1,0:T(2,128)(2,1)S(1)} async-done(((bf16[128,9,2,128]{3,2,1,0:T(2,128)(2,1)}), bf16[128,9,2,128]{3,2,1,0:T(2,128)(2,1)S(1)}, u32[]{:S(2)}, u32[]{:S(2)}) %all-to-all-start) | async-done | bytes 589856 | tf_op jit(solution)/shard_map/all_to_all | solution.py:215
  39.6 1.4 %gather_blocks.1 = bf16[128,9,2,128]{3,2,1,0:T(2,128)(2,1)} custom-call(s32[128]{0:T(128)S(1)} %dynamic-slice_bitcast_fusion.sources, bf16[128,9,2,128]{3,2,1,0:T(2,128)(2,1)S(1)} %all-to-all-done.blocks), custom_call_target="tpu_custom_call" | custom-call | tf_op jit(solution)/shard_map/gather_blocks/pallas_call | solution.py:113
  41.0 7.2 %all-to-all-start.1 = ((bf16[128,9,2,128]{3,2,1,0:T(2,128)(2,1)}), bf16[128,9,2,128]{3,2,1,0:T(2,128)(2,1)S(1)}, u32[]{:S(2)}, u32[]{:S(2)}) async-start(bf16[128,9,2,128]{3,2,1,0:T(2,128)(2,1)} %gather_blocks.1), calls=%async_computation.1 | async-start | bytes 1179648 | tf_op jit(solution)/shard_map/all_to_all | solution.py:219
  48.2 0.6 dynamic_slice.9
  50.4 0.0 copy-done.6
  50.4 0.6 dynamic_slice.10
  51.0 16.8 %all-to-all-done.1 = bf16[128,9,2,128]{3,2,1,0:T(2,128)(2,1)S(1)} async-done(((bf16[128,9,2,128]{3,2,1,0:T(2,128)(2,1)}), bf16[128,9,2,128]{3,2,1,0:T(2,128)(2,1)S(1)}, u32[]{:S(2)}, u32[]{:S(2)}) %all-to-all-start.1) | async-done | bytes 589856 | tf_op jit(solution)/shard_map/all_to_all | solution.py:219
  67.8 2.6 %arrived_attention.1 = bf16[1024,2,2,128]{3,2,1,0:T(2,128)(2,1)} custom-call(s32[1]{0:T(128)} %bitcast.1.length, bf16[256,576]{1,0:T(8,128)(2,1)S(1)} %get-tuple-element.11.queries, bf16[128,576]{1,0:T(8,128)(2,1)S(1)} %get-tuple-element.12.latents, bf16[2304,128]{1,0:T(8,128)(2,1)S(1)} %bitcast.9, ...), custom_call_target="tpu_custom_call", output_to_operand_aliasing={{}: (5, {})} | custom-call | tf_op jit(solution)/shard_map/arrived_attention/pallas_call | solution.py:192
  (3 shorter events, 0.0 us)
Async XLA Ops:
  0.0 1.3 %copy-start = (bf16[1,294912]{1,0:T(2,128)(2,1)S(1)}, bf16[1,294912]{1,0:T(2,128)(2,1)}, u32[]{:S(2)}) copy-start(bf16[1,294912]{1,0:T(2,128)(2,1)} %src.1) | copy-start | bytes 1769476
  1.3 17.5 %copy-start.2 = (bf16[4,147456]{1,0:T(4,128)(2,1)S(1)}, bf16[4,147456]{1,0:T(4,128)(2,1)}, u32[]{:S(2)}) copy-start(bf16[4,147456]{1,0:T(4,128)(2,1)} %queries.1) | copy-start | bytes 3538948
  1.3 17.5 %copy-start.3 = (bf16[4,1152]{1,0:T(4,128)(2,1)S(1)}, bf16[4,1152]{1,0:T(4,128)(2,1)}, u32[]{:S(2)}) copy-start(bf16[4,1152]{1,0:T(4,128)(2,1)} %new.1) | copy-start | bytes 27652
  1.3 17.5 %copy-start.4 = (s32[3]{0:T(128)S(1)}, s32[3]{0:T(128)}, u32[]{:S(2)}) copy-start(s32[3]{0:T(128)} %lengths.1) | copy-start | bytes 40
  1.5 2.2 %collective-permute-start = (bf16[2304,128]{1,0:T(8,128)(2,1)S(1)}, bf16[2304,128]{1,0:T(8,128)(2,1)}, u32[]{:S(2)}, u32[]{:S(2)}) collective-permute-start(bf16[2304,128]{1,0:T(8,128)(2,1)S(1)} %fresh_tiles.1), channel_id=1, source_target_pairs={{0,128},{128,0},{1,129},{129,1},{2,130},{130,2},{3,131},{131,3},{4... | collective-permute-start | bytes 1769480 | tf_op jit(solution)/shard_map/ppermute | solution.py:213
  3.8 35.8 %all-to-all-start = ((bf16[128,9,2,128]{3,2,1,0:T(2,128)(2,1)}), bf16[128,9,2,128]{3,2,1,0:T(2,128)(2,1)S(1)}, u32[]{:S(2)}, u32[]{:S(2)}) async-start(bf16[128,9,2,128]{3,2,1,0:T(2,128)(2,1)} %bitcast.3), calls=%async_computation | async-start | bytes 1179648 | tf_op jit(solution)/shard_map/all_to_all | solution.py:215
  18.8 1.7 %copy-start.1 = (bf16[3,294912]{1,0:T(4,128)(2,1)S(1)}, bf16[3,294912]{1,0:T(4,128)(2,1)}, u32[]{:S(2)}) copy-start(bf16[3,294912]{1,0:T(4,128)(2,1)} %caches.1) | copy-start | bytes 5308420
  20.5 8.0 %copy-start.5 = (s32[2,128]{1,0:T(2,128)S(1)}, s32[2,128]{1,0:T(2,128)}, u32[]{:S(2)}) copy-start(s32[2,128]{1,0:T(2,128)} %param.13) | copy-start | bytes 3076
  39.6 10.8 %copy-start.6 = (s32[2,128]{1,0:T(2,128)S(1)}, s32[2,128]{1,0:T(2,128)}, u32[]{:S(2)}) copy-start(s32[2,128]{1,0:T(2,128)} %param.12) | copy-start | bytes 3076
  41.0 26.7 %all-to-all-start.1 = ((bf16[128,9,2,128]{3,2,1,0:T(2,128)(2,1)}), bf16[128,9,2,128]{3,2,1,0:T(2,128)(2,1)S(1)}, u32[]{:S(2)}, u32[]{:S(2)}) async-start(bf16[128,9,2,128]{3,2,1,0:T(2,128)(2,1)} %gather_blocks.1), calls=%async_computation.1 | async-start | bytes 1179648 | tf_op jit(solution)/shard_map/all_to_all | solution.py:219

commit v3 on v2

--- a/solution.py
+++ b/solution.py
@@ -17,7 +17,6 @@
 CACHE_ROWS = CTX * KV // LANES
 QUERY_ROWS = STEPS * HEADS * KV // LANES
 CHUNKS = STEPS * HEADS * LAT // LANES
-GATHER_PIECES = 4
 BF, F32 = jnp.bfloat16, jnp.float32
 
 score_scale = 192.0 ** (-0.5)
@@ -53,13 +52,18 @@
     return jnp.concatenate([x[s * half : (s + 1) * half] for s in range(STEPS) for x in (even, odd)], axis=0)
 
 
-def probabilities(queries, keys, length):
+def penalty(length):
+    column = lax.broadcasted_iota(jnp.int32, (8, CTX + LANES), 1)
+    position = jnp.where(column < PAIRS, 2 * column, 2 * (column - PAIRS) + 1)
+    step = lax.broadcasted_iota(jnp.int32, (8, CTX + LANES), 0)
+    live = jnp.where(column < CTX, position, column - CTX) < jnp.where(column < CTX, length, step + 1)
+    return jnp.where(live, 0.0, -jnp.inf).astype(F32)
+
+
+def probabilities(queries, keys, penalties):
     scores = lax.dot_general(queries, keys, (((1,), (1,)), ((), ())), preferred_element_type=F32) * score_scale
-    column = lax.broadcasted_iota(jnp.int32, (1, CTX + LANES), 1)
-    position = jnp.where(column < PAIRS, 2 * column, 2 * (column - PAIRS) + 1)
-    step = lax.broadcasted_iota(jnp.int32, (STEPS * HEADS, 1), 0) >> (HEADS - 1).bit_length()
-    live = jnp.where(column < CTX, position, column - CTX) < jnp.where(column < CTX, length, step + 1)
-    scores = jnp.where(live, scores, -jnp.inf)
+    rows = [scores[s * HEADS : (s + 1) * HEADS] + penalties[s : s + 1] for s in range(STEPS)]
+    scores = jnp.concatenate(rows, axis=0)
     exps = jnp.exp(scores - jnp.max(scores, axis=1, keepdims=True))
     return (exps * (1.0 / jnp.sum(exps, axis=1, keepdims=True))).astype(BF)
 
@@ -95,18 +99,9 @@
     )(fresh)
 
 
-def gather_kernel(sources, blocks, out, picked, sems):
-    size = out.shape[0] // GATHER_PIECES
-    copies = []
-    for piece in range(GATHER_PIECES):
-        at = piece * size
-        for d in range(at, at + size):
-            picked[d] = blocks[sources[d]]
-        copy = pltpu.make_async_copy(picked.at[pl.ds(at, size)], out.at[pl.ds(at, size)], sems.at[piece])
-        copy.start()
-        copies.append(copy)
-    for copy in copies:
-        copy.wait()
+def gather_kernel(sources, blocks, out):
+    for d in range(out.shape[0]):
+        out[d] = blocks[sources[d]]
 
 
 def gather_blocks(sources, blocks):
@@ -114,15 +109,34 @@
         gather_kernel,
         out_shape=jax.ShapeDtypeStruct(blocks.shape, BF),
         in_specs=[in_smem, in_vmem],
-        out_specs=pl.BlockSpec(memory_space=pl.ANY),
-        scratch_shapes=[pltpu.VMEM(blocks.shape, BF), pltpu.SemaphoreType.DMA((GATHER_PIECES,))],
+        out_specs=in_vmem,
         compiler_params=small,
         name="gather_blocks",
     )(sources, blocks)
 
 
+def pair_rows(both, rows, place):
+    for c in range(place.start, place.start + place.size, LANES):
+        rows[pl.ds(c, LANES)] = both[pl.ds(2 * c, 2 * LANES), :].astype(BF).reshape(LANES, 2, LANES)
+
+
 def resident_kernel(
-    lengths, queries, new, caches, out, third, last_queries, last_latents, query_flat, cache_flat, rows
+    lengths,
+    fresh_lengths,
+    matching,
+    queries,
+    new,
+    caches,
+    out,
+    third,
+    last_queries,
+    last_latents,
+    last_penalty,
+    query_flat,
+    cache_flat,
+    both,
+    rows,
+    sem,
 ):
     def queries_of(row):
         flat_row(queries, row, query_flat, QUERY_ROWS)
@@ -131,19 +145,22 @@
     for r in range(ROWS - 1):
         flat_row(caches, r, cache_flat, CACHE_ROWS)
         keys = jnp.concatenate([*strided_halves(cache_flat, PAIRS), padded_latents(new, r)], axis=0)
-        probs = probabilities(queries_of(r), keys, lengths[r])
+        probs = probabilities(queries_of(r), keys, penalty(lengths[r]))
         context = jnp.dot(probs, keys[:, :LAT], preferred_element_type=F32)
         for step in range(STEPS):
-            put_context(rows, r, step, context[step * HEADS : (step + 1) * HEADS])
-    for c in range(0, CHUNKS, LANES):
-        piece = rows[pl.ds(c * ROWS, LANES * ROWS), :]
-        out[pl.ds(c, LANES)] = piece.astype(BF).reshape(LANES, 2, 2, LANES)
-    third[...] = rows[pl.ds(ROWS - 2, CHUNKS, ROWS), :]
+            put_context(both if r < 2 else third, r, step, context[step * HEADS : (step + 1) * HEADS])
+        if r == 1:
+            pair_rows(both, rows, pl.ds(0, CHUNKS))
+            copy = pltpu.make_async_copy(rows, out.at[:, 0], sem)
+            copy.start()
     last_queries[...] = queries_of(ROWS - 1)
     last_latents[...] = padded_latents(new, ROWS - 1)
-
-
-def resident_attention(lengths, queries, new, caches):
+    pool = lax.axis_index("pool")
+    last_penalty[...] = penalty(fresh_lengths[1 - pool, matching[pool, lax.axis_index("ep")]])
+    copy.wait()
+
+
+def resident_attention(lengths, fresh_lengths, matching, queries, new, caches):
     return pl.pallas_call(
         resident_kernel,
         out_shape=(
@@ -151,26 +168,29 @@
             jax.ShapeDtypeStruct((CHUNKS, LANES), F32),
             jax.ShapeDtypeStruct((STEPS * HEADS, KV), BF),
             jax.ShapeDtypeStruct((LANES, KV), BF),
+            jax.ShapeDtypeStruct((8, CTX + LANES), F32),
         ),
-        in_specs=[in_smem, in_vmem, in_vmem, in_vmem],
-        out_specs=(in_vmem,) * 4,
+        in_specs=[in_smem] * 3 + [in_vmem] * 3,
+        out_specs=(pl.BlockSpec(memory_space=pl.ANY),) + (in_vmem,) * 4,
         scratch_shapes=[
             pltpu.VMEM((QUERY_ROWS, LANES), F32),
             pltpu.VMEM((CACHE_ROWS, LANES), F32),
-            pltpu.VMEM((ROWS * CHUNKS, LANES), F32),
+            pltpu.VMEM((2 * CHUNKS, LANES), F32),
+            pltpu.VMEM((CHUNKS, 2, LANES), BF),
+            pltpu.SemaphoreType.DMA(()),
         ],
         compiler_params=pltpu.CompilerParams(vmem_limit_bytes=32 << 20),
         cost_estimate=pl.CostEstimate(flops=10**9, bytes_accessed=8 << 20, transcendentals=400000),
         name="resident_attention",
-    )(lengths, queries, new, caches)
-
-
-def arrived_kernel(length, queries, latents, tiles, third, before, out, both, rows, sems):
+    )(lengths, fresh_lengths, matching, queries, new, caches)
+
+
+def arrived_kernel(penalties, queries, latents, tiles, third, before, out, both, rows, sems):
     parts = tiles[...].reshape(PAIRS // 16, PAIR_ROWS, 16, LANES)
     halved = halves([parts[:, j].reshape(PAIRS, LANES) for j in range(PAIR_ROWS)])
     keys = jnp.concatenate([*halved, latents[...]], axis=0)
     both[pl.ds(0, CHUNKS, 2), :] = third[...]
-    probs = probabilities(queries[...], keys, length[0])
+    probs = probabilities(queries[...], keys, penalties[...])
     values = keys[:, :LAT]
     copies = []
     size = CHUNKS // STEPS
@@ -178,8 +198,7 @@
         context = jnp.dot(probs[step * HEADS : (step + 1) * HEADS], values, preferred_element_type=F32)
         put_context(both, ROWS - 1, step, context)
         place = pl.ds(step * size, size)
-        for c in range(step * size, (step + 1) * size, LANES):
-            rows[pl.ds(c, LANES)] = both[pl.ds(2 * c, 2 * LANES), :].astype(BF).reshape(LANES, 2, LANES)
+        pair_rows(both, rows, place)
         copy = pltpu.make_async_copy(rows.at[place], out.at[place, 1], sems.at[step])
         copy.start()
         copies.append(copy)
@@ -187,12 +206,12 @@
         copy.wait()
 
 
-def arrived_attention(length, queries, latents, tiles, third, before):
+def arrived_attention(penalties, queries, latents, tiles, third, before):
     whole = pl.BlockSpec(memory_space=pl.ANY)
     return pl.pallas_call(
         arrived_kernel,
         out_shape=jax.ShapeDtypeStruct(before.shape, BF),
-        in_specs=[in_smem, in_vmem, in_vmem, in_vmem, in_vmem, whole],
+        in_specs=[in_vmem] * 5 + [whole],
         out_specs=whole,
         scratch_shapes=[
             pltpu.VMEM((2 * CHUNKS, LANES), F32),
@@ -202,7 +221,7 @@
         input_output_aliases={5: 0},
         compiler_params=pltpu.CompilerParams(vmem_limit_bytes=24 << 20),
         name="arrived_attention",
-    )(length, queries, latents, tiles, third, before)
+    )(penalties, queries, latents, tiles, third, before)
 
 
 def per_device(queries, new_latent, resident_cache, resident_len, fresh_cache, fresh_len, matching):
@@ -213,13 +232,14 @@
     tiles = lax.ppermute(tiles, "pool", [(0, 1), (1, 0)])
     blocks = tiles.reshape(group_count, PAIR_ROWS, 2, LANES)
     blocks = lax.all_to_all(blocks, "ep", split_axis=0, concat_axis=0, tiled=True)
-    out, third, last_queries, last_latents = resident_attention(resident_len, queries, new_latent, resident_cache)
+    out, third, last_queries, last_latents, penalties = resident_attention(
+        resident_len, fresh_len, matching, queries, new_latent, resident_cache
+    )
     blocks, third = lax.optimization_barrier((blocks, third))
     blocks = gather_blocks(own_sources, blocks)
     blocks = lax.all_to_all(blocks, "ep", split_axis=0, concat_axis=0, tiled=True)
-    arrive_len = fresh_len[1 - pool_index, own_sources[lax.axis_index("ep")]]
     tiles = blocks.reshape(CACHE_ROWS, LANES)
-    out = arrived_attention(arrive_len[None], last_queries, last_latents, tiles, third, out)
+    out = arrived_attention(penalties, last_queries, last_latents, tiles, third, out)
     return out.transpose(1, 2, 0, 3).reshape(ROWS, -1)
 
 

time: 70.7 us -> 69.2 us (0.979)
  blocking collectives: 0 us -> 26.5 us
  waiting for transfers between devices: 30 us -> 14.2 us
  starting transfers between devices: 22.3 us -> 15.1 us
  Pallas kernels: 12.3 us -> 10.1 us
  between operations: 1.75 us -> 0.11 us
  local copies, waits for them, and re-layouts: 4.08 us -> 2.96 us
    all_to_all x0 -> x1, blocking collectives: none -> 26.5 us  [per_device(): lax.all_to_all(blocks, 'ep', split_axis=0, concat_axis=0, tiled=True)]
    all_to_all x2 -> x1, waiting for transfers between devices: 27.9 us -> 12 us  [per_device(): lax.all_to_all(blocks, 'ep', split_axis=0, concat_axis=0, tiled=True)]
    all_to_all x2 -> x1, starting transfers between devices: 22.2 us -> 15 us  [per_device(): lax.all_to_all(blocks, 'ep', split_axis=0, concat_axis=0, tiled=True)]
    dynamic_slice x2 -> x0, local copies, waits for them, and re-layouts: 1.12 us -> none  [per_device(): arrive_len = fresh_len[1 - pool_index, own_sources[lax.axis_index('ep')]]]
    pallas_call x1, Pallas kernels: 8.01 us -> 7.04 us  [resident_attention(): pl.pallas_call(resident_kernel, out_shape=(jax.ShapeDtypeStruct((CHUNKS,...]
    pallas_call x1, Pallas kernels: 1.43 us -> 0.66 us  [gather_blocks(): pl.pallas_call(gather_kernel, out_shape=jax.ShapeDtypeStruct(blocks.shape...]
  transfers between devices with their start and end apart: 3 -> 2, of which waited for: 3 -> 2; matrix products, arithmetic and copies ran while one was open for 2% -> 0% of each run, Pallas kernels for 11% -> 10%
where the time goes in v3:
time: 69.2 us; the launch traced here: 68.9 us
  blocking collectives  26.5 us (38%)
  starting transfers between devices  15.1 us (22%)
  waiting for transfers between devices  14.2 us (21%)
  Pallas kernels  10.1 us (15%)
  local copies, waits for them, and re-layouts  2.96 us (4%)
    all_to_all x1, blocking collectives, per_device(): lax.all_to_all(blocks, 'ep', split_axis=0, concat_axis=0, tiled=True)  26.5 us
    all_to_all x1, starting transfers between devices, per_device(): lax.all_to_all(blocks, 'ep', split_axis=0, concat_axis=0, tiled=True)  15 us
    all_to_all x1, waiting for transfers between devices, per_device(): lax.all_to_all(blocks, 'ep', split_axis=0, concat_axis=0, tiled=True)  12 us
    pallas_call x1, Pallas kernels, resident_attention(): pl.pallas_call(resident_kernel, out_shape=(jax.ShapeDtypeStruct((CHUNKS,...  7.04 us
    unnamed x14, local copies, waits for them, and re-layouts  2.95 us
    ppermute x1, waiting for transfers between devices, per_device(): tiles = lax.ppermute(tiles, 'pool', [(0, 1), (1, 0)])  2.12 us
    pallas_call x1, Pallas kernels, arrived_attention(): pl.pallas_call(arrived_kernel, out_shape=jax.ShapeDtypeStruct(before.shap...  2.09 us
  transfers between devices with their start and end apart: 2, of which 2 were waited for; matrix products, arithmetic and copies ran while one was open for 0% of the time, Pallas kernels for 10%

profile of v3, /device:TPU:32, one launch (start us, length us, event | category | flops | bytes accessed | tf_op | source)
XLA Modules:
  0.0 68.9 jit_solution(16648729175212546249)
XLA Ops:
  0.0 0.0 copy-start
  0.0 1.3 %copy-done = bf16[1,294912]{1,0:T(2,128)(2,1)S(1)} copy-done((bf16[1,294912]{1,0:T(2,128)(2,1)S(1)}, bf16[1,294912]{1,0:T(2,128)(2,1)}, u32[]{:S(2)}) %copy-start) | copy-done | bytes 589848
  1.3 0.0 copy-start.2
  1.3 0.0 copy-start.3
  1.3 0.0 copy-start.4
  1.3 0.0 copy-start.5
  1.3 0.0 copy-start.6
  1.3 0.3 fresh_tiles.1
  1.6 0.1 collective-permute-start
  1.7 2.1 %collective-permute-done = bf16[2304,128]{1,0:T(8,128)(2,1)} collective-permute-done((bf16[2304,128]{1,0:T(8,128)(2,1)S(1)}, bf16[2304,128]{1,0:T(8,128)(2,1)}, u32[]{:S(2)}, u32[]{:S(2)}) %collective-permute-start) | collective-permute-done | bytes 589856 | tf_op jit(solution)/shard_map/ppermute | solution.py:232
  3.8 15.0 %all-to-all-start = ((bf16[128,9,2,128]{3,2,1,0:T(2,128)(2,1)}), bf16[128,9,2,128]{3,2,1,0:T(2,128)(2,1)S(1)}, u32[]{:S(2)}, u32[]{:S(2)}) async-start(bf16[128,9,2,128]{3,2,1,0:T(2,128)(2,1)} %bitcast.1), calls=%async_computation | async-start | bytes 1179648 | tf_op jit(solution)/shard_map/all_to_all | solution.py:234
  18.8 0.0 copy-done.2
  18.8 0.0 copy-done.3
  18.8 0.0 copy-done.4
  18.8 0.0 copy-done.5
  18.8 0.0 copy-done.6
  18.8 0.0 copy-start.1
  18.9 1.7 %copy-done.1 = bf16[3,294912]{1,0:T(4,128)(2,1)S(1)} copy-done((bf16[3,294912]{1,0:T(4,128)(2,1)S(1)}, bf16[3,294912]{1,0:T(4,128)(2,1)}, u32[]{:S(2)}) %copy-start.1) | copy-done | bytes 1769496
  20.5 7.0 %resident_attention.1 = (bf16[1024,2,2,128]{3,2,1,0:T(2,128)(2,1)}, f32[1024,128]{1,0:T(8,128)S(1)}, bf16[256,576]{1,0:T(8,128)(2,1)S(1)}, bf16[128,576]{1,0:T(8,128)(2,1)S(1)}, f32[8,640]{1,0:T(8,128)S(1)}) custom-call(s32[3]{0:T(128)S(1)} %copy-done.6, s32[2,128]{1,0:T(2,128)S(1)} %copy-done.4, s32[2,128]{1,0:T(2,128)S(1)} %copy-done.5, ...), custom_call_target="tpu_custom_call" | custom-call | flops 1000000000 | bytes 8388608 | tf_op jit(solution)/shard_map/resident_attention/pallas_call | solution.py:164
  27.6 12.0 %all-to-all-done.blocks = bf16[128,9,2,128]{3,2,1,0:T(2,128)(2,1)S(1)} async-done(((bf16[128,9,2,128]{3,2,1,0:T(2,128)(2,1)}), bf16[128,9,2,128]{3,2,1,0:T(2,128)(2,1)S(1)}, u32[]{:S(2)}, u32[]{:S(2)}) %all-to-all-start) | async-done | bytes 589856 | tf_op jit(solution)/shard_map/all_to_all | solution.py:234
  39.6 0.7 gather_blocks.1
  40.3 26.5 %all_to_all.10 = bf16[128,9,2,128]{3,2,1,0:T(2,128)(2,1)S(1)} all-to-all(bf16[128,9,2,128]{3,2,1,0:T(2,128)(2,1)S(1)} %gather_blocks.1), channel_id=1, replica_groups=mesh['pool'=2,'ep'=128] {'ep'}, dimensions={0} | all-to-all | bytes 1179648 | tf_op jit(solution)/shard_map/all_to_all | solution.py:240
  66.8 2.1 %arrived_attention.1 = bf16[1024,2,2,128]{3,2,1,0:T(2,128)(2,1)} custom-call(f32[8,640]{1,0:T(8,128)S(1)} %get-tuple-element.12.penalties, bf16[256,576]{1,0:T(8,128)(2,1)S(1)} %get-tuple-element.13.queries, bf16[128,576]{1,0:T(8,128)(2,1)S(1)} %get-tuple-element.14.latents, bf16[2304,128]{1,0:T(8,128)(2,1)S(1)} %bitcast.7, ...), custom_call_target="tpu_custom_call", output_to_operand_aliasing={{}: (5, {})} | custom-call | tf_op jit(solution)/shard_map/arrived_attention/pallas_call | solution.py:211
  (1 shorter events, 0.0 us)
Async XLA Ops:
  0.0 1.3 %copy-start = (bf16[1,294912]{1,0:T(2,128)(2,1)S(1)}, bf16[1,294912]{1,0:T(2,128)(2,1)}, u32[]{:S(2)}) copy-start(bf16[1,294912]{1,0:T(2,128)(2,1)} %src.1) | copy-start | bytes 1769476
  1.3 17.5 %copy-start.2 = (bf16[4,147456]{1,0:T(4,128)(2,1)S(1)}, bf16[4,147456]{1,0:T(4,128)(2,1)}, u32[]{:S(2)}) copy-start(bf16[4,147456]{1,0:T(4,128)(2,1)} %queries.1) | copy-start | bytes 3538948
  1.3 17.5 %copy-start.3 = (bf16[4,1152]{1,0:T(4,128)(2,1)S(1)}, bf16[4,1152]{1,0:T(4,128)(2,1)}, u32[]{:S(2)}) copy-start(bf16[4,1152]{1,0:T(4,128)(2,1)} %new.1) | copy-start | bytes 27652
  1.3 17.5 %copy-start.4 = (s32[2,128]{1,0:T(2,128)S(1)}, s32[2,128]{1,0:T(2,128)}, u32[]{:S(2)}) copy-start(s32[2,128]{1,0:T(2,128)} %fresh_lengths.1) | copy-start | bytes 3076
  1.3 17.6 %copy-start.5 = (s32[2,128]{1,0:T(2,128)S(1)}, s32[2,128]{1,0:T(2,128)}, u32[]{:S(2)}) copy-start(s32[2,128]{1,0:T(2,128)} %matching.1) | copy-start | bytes 3076
  1.3 17.6 %copy-start.6 = (s32[3]{0:T(128)S(1)}, s32[3]{0:T(128)}, u32[]{:S(2)}) copy-start(s32[3]{0:T(128)} %lengths.1) | copy-start | bytes 40
  1.6 2.2 %collective-permute-start = (bf16[2304,128]{1,0:T(8,128)(2,1)S(1)}, bf16[2304,128]{1,0:T(8,128)(2,1)}, u32[]{:S(2)}, u32[]{:S(2)}) collective-permute-start(bf16[2304,128]{1,0:T(8,128)(2,1)S(1)} %fresh_tiles.1), channel_id=1, source_target_pairs={{0,128},{128,0},{1,129},{129,1},{2,130},{130,2},{3,131},{131,3},{4... | collective-permute-start | bytes 1769480 | tf_op jit(solution)/shard_map/ppermute | solution.py:232
  3.8 35.8 %all-to-all-start = ((bf16[128,9,2,128]{3,2,1,0:T(2,128)(2,1)}), bf16[128,9,2,128]{3,2,1,0:T(2,128)(2,1)S(1)}, u32[]{:S(2)}, u32[]{:S(2)}) async-start(bf16[128,9,2,128]{3,2,1,0:T(2,128)(2,1)} %bitcast.1), calls=%async_computation | async-start | bytes 1179648 | tf_op jit(solution)/shard_map/all_to_all | solution.py:234
  18.8 1.7 %copy-start.1 = (bf16[3,294912]{1,0:T(4,128)(2,1)S(1)}, bf16[3,294912]{1,0:T(4,128)(2,1)}, u32[]{:S(2)}) copy-start(bf16[3,294912]{1,0:T(4,128)(2,1)} %caches.1) | copy-start | bytes 5308420

commit v4 on v3

--- a/solution.py
+++ b/solution.py
@@ -100,8 +100,9 @@
 
 
 def gather_kernel(sources, blocks, out):
-    for d in range(out.shape[0]):
-        out[d] = blocks[sources[d]]
+    last = out.shape[0] - 1
+    for d in range(last + 1):
+        out[d] = blocks[last - sources[last - d]]
 
 
 def gather_blocks(sources, blocks):
@@ -224,6 +225,11 @@
     )(penalties, queries, latents, tiles, third, before)
 
 
+def exchange(blocks):
+    places = list(range(blocks.shape[0]))[::-1]
+    return lax.all_to_all(blocks, "ep", split_axis=0, concat_axis=0, tiled=True, axis_index_groups=[places])
+
+
 def per_device(queries, new_latent, resident_cache, resident_len, fresh_cache, fresh_len, matching):
     group_count = lax.axis_size("ep")
     pool_index = lax.axis_index("pool")
@@ -231,13 +237,13 @@
     tiles = fresh_tiles(fresh_cache)
     tiles = lax.ppermute(tiles, "pool", [(0, 1), (1, 0)])
     blocks = tiles.reshape(group_count, PAIR_ROWS, 2, LANES)
-    blocks = lax.all_to_all(blocks, "ep", split_axis=0, concat_axis=0, tiled=True)
+    blocks = exchange(blocks)
     out, third, last_queries, last_latents, penalties = resident_attention(
         resident_len, fresh_len, matching, queries, new_latent, resident_cache
     )
     blocks, third = lax.optimization_barrier((blocks, third))
     blocks = gather_blocks(own_sources, blocks)
-    blocks = lax.all_to_all(blocks, "ep", split_axis=0, concat_axis=0, tiled=True)
+    blocks = exchange(blocks)
     tiles = blocks.reshape(CACHE_ROWS, LANES)
     out = arrived_attention(penalties, last_queries, last_latents, tiles, third, out)
     return out.transpose(1, 2, 0, 3).reshape(ROWS, -1)

time: 69.2 us -> 66.2 us (0.957)
  waiting for transfers between devices: 14.2 us -> 8.92 us
  starting transfers between devices: 15.1 us -> 16.9 us
    all_to_all x1, waiting for transfers between devices: 12 us -> 6.8 us  [exchange(): lax.all_to_all(blocks, 'ep', split_axis=0, concat_axis=0, tiled=True, axi...]
    all_to_all x1, starting transfers between devices: 15 us -> 16.8 us  [exchange(): lax.all_to_all(blocks, 'ep', split_axis=0, concat_axis=0, tiled=True, axi...]
  transfers between devices with their start and end apart: 2 -> 2, of which waited for: 2 -> 2; matrix products, arithmetic and copies ran while one was open for 0% -> 0% of each run, Pallas kernels for 10% -> 11%
where the time goes in v4:
time: 66.2 us; the launch traced here: 65.5 us
  blocking collectives  26.6 us (40%)
  starting transfers between devices  16.9 us (26%)
  Pallas kernels  10 us (15%)
  waiting for transfers between devices  8.92 us (13%)
  local copies, waits for them, and re-layouts  2.96 us (4%)
    all_to_all x1, blocking collectives, exchange(): lax.all_to_all(blocks, 'ep', split_axis=0, concat_axis=0, tiled=True, axi...  26.6 us
    all_to_all x1, starting transfers between devices, exchange(): lax.all_to_all(blocks, 'ep', split_axis=0, concat_axis=0, tiled=True, axi...  16.8 us
    pallas_call x1, Pallas kernels, resident_attention(): pl.pallas_call(resident_kernel, out_shape=(jax.ShapeDtypeStruct((CHUNKS,...  7.02 us
    all_to_all x1, waiting for transfers between devices, exchange(): lax.all_to_all(blocks, 'ep', split_axis=0, concat_axis=0, tiled=True, axi...  6.8 us
    unnamed x14, local copies, waits for them, and re-layouts  2.95 us
    ppermute x1, waiting for transfers between devices, per_device(): tiles = lax.ppermute(tiles, 'pool', [(0, 1), (1, 0)])  2.12 us
    pallas_call x1, Pallas kernels, arrived_attention(): pl.pallas_call(arrived_kernel, out_shape=jax.ShapeDtypeStruct(before.shap...  2.08 us
  transfers between devices with their start and end apart: 2, of which 2 were waited for; matrix products, arithmetic and copies ran while one was open for 0% of the time, Pallas kernels for 11%

profile of v4, /device:TPU:32, one launch (start us, length us, event | category | flops | bytes accessed | tf_op | source)
XLA Modules:
  0.0 65.5 jit_solution(14468642248193935505)
XLA Ops:
  0.0 0.0 copy-start
  0.0 1.3 %copy-done = bf16[1,294912]{1,0:T(2,128)(2,1)S(1)} copy-done((bf16[1,294912]{1,0:T(2,128)(2,1)S(1)}, bf16[1,294912]{1,0:T(2,128)(2,1)}, u32[]{:S(2)}) %copy-start) | copy-done | bytes 589848
  1.3 0.0 copy-start.2
  1.3 0.0 copy-start.3
  1.3 0.0 copy-start.4
  1.3 0.0 copy-start.5
  1.3 0.0 copy-start.6
  1.3 0.3 fresh_tiles.1
  1.6 0.1 collective-permute-start
  1.7 2.1 %collective-permute-done = bf16[2304,128]{1,0:T(8,128)(2,1)} collective-permute-done((bf16[2304,128]{1,0:T(8,128)(2,1)S(1)}, bf16[2304,128]{1,0:T(8,128)(2,1)}, u32[]{:S(2)}, u32[]{:S(2)}) %collective-permute-start) | collective-permute-done | bytes 589856 | tf_op jit(solution)/shard_map/ppermute | solution.py:238
  3.8 16.8 %all-to-all-start = ((bf16[128,9,2,128]{3,2,1,0:T(2,128)(2,1)}), bf16[128,9,2,128]{3,2,1,0:T(2,128)(2,1)S(1)}, u32[]{:S(2)}, u32[]{:S(2)}) async-start(bf16[128,9,2,128]{3,2,1,0:T(2,128)(2,1)} %bitcast.1), calls=%async_computation | async-start | bytes 1179648 | tf_op jit(solution)/shard_map/all_to_all | solution.py:230
  20.6 0.0 copy-done.2
  20.6 0.0 copy-done.3
  20.6 0.0 copy-done.4
  20.6 0.0 copy-done.5
  20.6 0.0 copy-done.6
  20.6 0.0 copy-start.1
  20.6 1.7 %copy-done.1 = bf16[3,294912]{1,0:T(4,128)(2,1)S(1)} copy-done((bf16[3,294912]{1,0:T(4,128)(2,1)S(1)}, bf16[3,294912]{1,0:T(4,128)(2,1)}, u32[]{:S(2)}) %copy-start.1) | copy-done | bytes 1769496
  22.3 7.0 %resident_attention.1 = (bf16[1024,2,2,128]{3,2,1,0:T(2,128)(2,1)}, f32[1024,128]{1,0:T(8,128)S(1)}, bf16[256,576]{1,0:T(8,128)(2,1)S(1)}, bf16[128,576]{1,0:T(8,128)(2,1)S(1)}, f32[8,640]{1,0:T(8,128)S(1)}) custom-call(s32[3]{0:T(128)S(1)} %copy-done.6, s32[2,128]{1,0:T(2,128)S(1)} %copy-done.4, s32[2,128]{1,0:T(2,128)S(1)} %copy-done.5, ...), custom_call_target="tpu_custom_call" | custom-call | flops 1000000000 | bytes 8388608 | tf_op jit(solution)/shard_map/resident_attention/pallas_call | solution.py:165
  29.4 6.8 %all-to-all-done.blocks = bf16[128,9,2,128]{3,2,1,0:T(2,128)(2,1)S(1)} async-done(((bf16[128,9,2,128]{3,2,1,0:T(2,128)(2,1)}), bf16[128,9,2,128]{3,2,1,0:T(2,128)(2,1)S(1)}, u32[]{:S(2)}, u32[]{:S(2)}) %all-to-all-start) | async-done | bytes 589856 | tf_op jit(solution)/shard_map/all_to_all | solution.py:230
  36.2 0.7 %gather_blocks.1 = bf16[128,9,2,128]{3,2,1,0:T(2,128)(2,1)S(1)} custom-call(s32[128]{0:T(128)S(1)} %dynamic-slice_bitcast_fusion.sources, bf16[128,9,2,128]{3,2,1,0:T(2,128)(2,1)S(1)} %all-to-all-done.blocks), custom_call_target="tpu_custom_call" | custom-call | tf_op jit(solution)/shard_map/gather_blocks/pallas_call | solution.py:109
  36.8 26.6 %all_to_all.10 = bf16[128,9,2,128]{3,2,1,0:T(2,128)(2,1)S(1)} all-to-all(bf16[128,9,2,128]{3,2,1,0:T(2,128)(2,1)S(1)} %gather_blocks.1), channel_id=1, replica_groups={{127,126,125,124,123,122,121,120,119,118,117,116,115,114,113,112,111,11..., dimensions={0} | all-to-all | bytes 1179648 | tf_op jit(solution)/shard_map/all_to_all | solution.py:230
  63.5 2.1 %arrived_attention.1 = bf16[1024,2,2,128]{3,2,1,0:T(2,128)(2,1)} custom-call(f32[8,640]{1,0:T(8,128)S(1)} %get-tuple-element.12.penalties, bf16[256,576]{1,0:T(8,128)(2,1)S(1)} %get-tuple-element.13.queries, bf16[128,576]{1,0:T(8,128)(2,1)S(1)} %get-tuple-element.14.latents, bf16[2304,128]{1,0:T(8,128)(2,1)S(1)} %bitcast.7, ...), custom_call_target="tpu_custom_call", output_to_operand_aliasing={{}: (5, {})} | custom-call | tf_op jit(solution)/shard_map/arrived_attention/pallas_call | solution.py:212
  (1 shorter events, 0.0 us)
Async XLA Ops:
  0.0 1.3 %copy-start = (bf16[1,294912]{1,0:T(2,128)(2,1)S(1)}, bf16[1,294912]{1,0:T(2,128)(2,1)}, u32[]{:S(2)}) copy-start(bf16[1,294912]{1,0:T(2,128)(2,1)} %src.1) | copy-start | bytes 1769476
  1.3 19.3 %copy-start.2 = (bf16[4,147456]{1,0:T(4,128)(2,1)S(1)}, bf16[4,147456]{1,0:T(4,128)(2,1)}, u32[]{:S(2)}) copy-start(bf16[4,147456]{1,0:T(4,128)(2,1)} %queries.1) | copy-start | bytes 3538948
  1.3 19.3 %copy-start.3 = (bf16[4,1152]{1,0:T(4,128)(2,1)S(1)}, bf16[4,1152]{1,0:T(4,128)(2,1)}, u32[]{:S(2)}) copy-start(bf16[4,1152]{1,0:T(4,128)(2,1)} %new.1) | copy-start | bytes 27652
  1.3 19.3 %copy-start.4 = (s32[2,128]{1,0:T(2,128)S(1)}, s32[2,128]{1,0:T(2,128)}, u32[]{:S(2)}) copy-start(s32[2,128]{1,0:T(2,128)} %fresh_lengths.1) | copy-start | bytes 3076
  1.3 19.3 %copy-start.5 = (s32[2,128]{1,0:T(2,128)S(1)}, s32[2,128]{1,0:T(2,128)}, u32[]{:S(2)}) copy-start(s32[2,128]{1,0:T(2,128)} %matching.1) | copy-start | bytes 3076
  1.3 19.3 %copy-start.6 = (s32[3]{0:T(128)S(1)}, s32[3]{0:T(128)}, u32[]{:S(2)}) copy-start(s32[3]{0:T(128)} %lengths.1) | copy-start | bytes 40
  1.6 2.2 %collective-permute-start = (bf16[2304,128]{1,0:T(8,128)(2,1)S(1)}, bf16[2304,128]{1,0:T(8,128)(2,1)}, u32[]{:S(2)}, u32[]{:S(2)}) collective-permute-start(bf16[2304,128]{1,0:T(8,128)(2,1)S(1)} %fresh_tiles.1), channel_id=1, source_target_pairs={{0,128},{128,0},{1,129},{129,1},{2,130},{130,2},{3,131},{131,3},{4... | collective-permute-start | bytes 1769480 | tf_op jit(solution)/shard_map/ppermute | solution.py:238
  3.8 32.4 %all-to-all-start = ((bf16[128,9,2,128]{3,2,1,0:T(2,128)(2,1)}), bf16[128,9,2,128]{3,2,1,0:T(2,128)(2,1)S(1)}, u32[]{:S(2)}, u32[]{:S(2)}) async-start(bf16[128,9,2,128]{3,2,1,0:T(2,128)(2,1)} %bitcast.1), calls=%async_computation | async-start | bytes 1179648 | tf_op jit(solution)/shard_map/all_to_all | solution.py:230
  20.6 1.7 %copy-start.1 = (bf16[3,294912]{1,0:T(4,128)(2,1)S(1)}, bf16[3,294912]{1,0:T(4,128)(2,1)}, u32[]{:S(2)}) copy-start(bf16[3,294912]{1,0:T(4,128)(2,1)} %caches.1) | copy-start | bytes 5308420

commit v5 on v4

--- a/solution.py
+++ b/solution.py
@@ -79,15 +79,27 @@
             ]
 
 
-def fresh_kernel(src, out, flat):
-    flat_row(src, 0, flat, CACHE_ROWS)
+def cut_tiles(flat, out):
     for g in range(PAIRS // 16):
         for j in range(PAIR_ROWS):
             tile = flat[pl.ds(g * 16 * PAIR_ROWS + j, 16, PAIR_ROWS), :]
             out[pl.ds((g * PAIR_ROWS + j) * 16, 16), :] = tile.astype(BF)
 
 
-def fresh_tiles(fresh):
+def fresh_kernel(src, out, flat):
+    flat_row(src, 0, flat, CACHE_ROWS)
+    pool = lax.axis_index("pool")
+
+    @pl.when(pool == 0)
+    def _():
+        cut_tiles(flat, out)
+
+    @pl.when(pool == 1)
+    def _():
+        out[...] = flat[...].astype(BF)
+
+
+def fresh_rows(fresh):
     return pl.pallas_call(
         fresh_kernel,
         out_shape=jax.ShapeDtypeStruct((CACHE_ROWS, LANES), BF),
@@ -95,8 +107,39 @@
         out_specs=in_vmem,
         scratch_shapes=[pltpu.VMEM((CACHE_ROWS, LANES), F32)],
         compiler_params=small,
-        name="fresh_tiles",
+        name="fresh_rows",
     )(fresh)
+
+
+def taken_kernel(rows, out, plain, flat, cut, sems):
+    @pl.when(lax.axis_index("pool") == 0)
+    def _():
+        load = pltpu.make_async_copy(rows, plain, sems.at[0])
+        load.start()
+        load.wait()
+        flat[...] = plain[...].astype(F32)
+        cut_tiles(flat, cut)
+        store = pltpu.make_async_copy(cut, out, sems.at[1])
+        store.start()
+        store.wait()
+
+
+def taken_tiles(rows):
+    return pl.pallas_call(
+        taken_kernel,
+        out_shape=jax.ShapeDtypeStruct(rows.shape, BF),
+        in_specs=[pl.BlockSpec(memory_space=pl.ANY)],
+        out_specs=pl.BlockSpec(memory_space=pl.ANY),
+        scratch_shapes=[
+            pltpu.VMEM((CACHE_ROWS, LANES), BF),
+            pltpu.VMEM((CACHE_ROWS, LANES), F32),
+            pltpu.VMEM((CACHE_ROWS, LANES), BF),
+            pltpu.SemaphoreType.DMA((2,)),
+        ],
+        input_output_aliases={0: 0},
+        compiler_params=small,
+        name="taken_tiles",
+    )(rows)
 
 
 def gather_kernel(sources, blocks, out):
@@ -234,8 +277,7 @@
     group_count = lax.axis_size("ep")
     pool_index = lax.axis_index("pool")
     own_sources = matching[pool_index]
-    tiles = fresh_tiles(fresh_cache)
-    tiles = lax.ppermute(tiles, "pool", [(0, 1), (1, 0)])
+    tiles = taken_tiles(lax.ppermute(fresh_rows(fresh_cache), "pool", [(0, 1), (1, 0)]))
     blocks = tiles.reshape(group_count, PAIR_ROWS, 2, LANES)
     blocks = exchange(blocks)
     out, third, last_queries, last_latents, penalties = resident_attention(

time: 66.2 us -> 64.8 us (0.979)
  Pallas kernels: 10 us -> 12.1 us
  waiting for transfers between devices: 8.92 us -> 6.96 us
  blocking collectives: 26.6 us -> 25 us
    pallas_call x1 -> x2, Pallas kernels: 0.26 us -> 2.29 us  [the longest x1 2.03 us: taken_tiles(): pl.pallas_call(taken_kernel, out_shape=jax.ShapeDtypeStruct(rows.shape, B...]
    all_to_all x1, waiting for transfers between devices: 6.8 us -> 4.83 us  [exchange(): lax.all_to_all(blocks, 'ep', split_axis=0, concat_axis=0, tiled=True, axi...]
    all_to_all x1, blocking collectives: 26.6 us -> 25 us  [exchange(): lax.all_to_all(blocks, 'ep', split_axis=0, concat_axis=0, tiled=True, axi...]
where the time goes in v5:
time: 64.8 us; the launch traced here: 64.1 us
  blocking collectives  25 us (39%)
  starting transfers between devices  16.9 us (26%)
  Pallas kernels  12.1 us (19%)
  waiting for transfers between devices  6.96 us (11%)
  local copies, waits for them, and re-layouts  2.97 us (5%)
    all_to_all x1, blocking collectives, exchange(): lax.all_to_all(blocks, 'ep', split_axis=0, concat_axis=0, tiled=True, axi...  25 us
    all_to_all x1, starting transfers between devices, exchange(): lax.all_to_all(blocks, 'ep', split_axis=0, concat_axis=0, tiled=True, axi...  16.8 us
    pallas_call x1, Pallas kernels, resident_attention(): pl.pallas_call(resident_kernel, out_shape=(jax.ShapeDtypeStruct((CHUNKS,...  7.01 us
    all_to_all x1, waiting for transfers between devices, exchange(): lax.all_to_all(blocks, 'ep', split_axis=0, concat_axis=0, tiled=True, axi...  4.83 us
    unnamed x14, local copies, waits for them, and re-layouts  2.96 us
    ppermute x1, waiting for transfers between devices, per_device(): lax.ppermute(fresh_rows(fresh_cache), 'pool', [(0, 1), (1, 0)])  2.12 us
    pallas_call x1, Pallas kernels, arrived_attention(): pl.pallas_call(arrived_kernel, out_shape=jax.ShapeDtypeStruct(before.shap...  2.08 us
    pallas_call x1, Pallas kernels, taken_tiles(): pl.pallas_call(taken_kernel, out_shape=jax.ShapeDtypeStruct(rows.shape, B...  2.03 us
  transfers between devices with their start and end apart: 2, of which 2 were waited for; matrix products, arithmetic and copies ran while one was open for 0% of the time, Pallas kernels for 11%

profile of v5, /device:TPU:32, one launch (start us, length us, event | category | flops | bytes accessed | tf_op | source)
XLA Modules:
  0.0 64.1 jit_solution(14097018052480159222)
XLA Ops:
  0.0 0.0 copy-start
  0.0 1.3 %copy-done = bf16[1,294912]{1,0:T(2,128)(2,1)S(1)} copy-done((bf16[1,294912]{1,0:T(2,128)(2,1)S(1)}, bf16[1,294912]{1,0:T(2,128)(2,1)}, u32[]{:S(2)}) %copy-start) | copy-done | bytes 589848
  1.3 0.3 fresh_rows.1
  1.5 0.0 copy-start.2
  1.6 0.0 copy-start.3
  1.6 0.0 copy-start.4
  1.6 0.0 copy-start.5
  1.6 0.0 copy-start.6
  1.6 0.1 collective-permute-start
  1.7 2.1 %collective-permute-done.rows = bf16[2304,128]{1,0:T(8,128)(2,1)} collective-permute-done((bf16[2304,128]{1,0:T(8,128)(2,1)S(1)}, bf16[2304,128]{1,0:T(8,128)(2,1)}, u32[]{:S(2)}, u32[]{:S(2)}) %collective-permute-start) | collective-permute-done | bytes 589856 | tf_op jit(solution)/shard_map/ppermute | solution.py:280
  3.8 2.0 %taken_tiles.1 = bf16[2304,128]{1,0:T(8,128)(2,1)} custom-call(bf16[2304,128]{1,0:T(8,128)(2,1)} %collective-permute-done.rows), custom_call_target="tpu_custom_call", output_to_operand_aliasing={{}: (0, {})} | custom-call | tf_op jit(solution)/shard_map/taken_tiles/pallas_call | solution.py:128
  5.9 16.8 %all-to-all-start = ((bf16[128,9,2,128]{3,2,1,0:T(2,128)(2,1)}), bf16[128,9,2,128]{3,2,1,0:T(2,128)(2,1)S(1)}, u32[]{:S(2)}, u32[]{:S(2)}) async-start(bf16[128,9,2,128]{3,2,1,0:T(2,128)(2,1)} %bitcast.1), calls=%async_computation | async-start | bytes 1179648 | tf_op jit(solution)/shard_map/all_to_all | solution.py:273
  22.7 0.0 copy-done.2
  22.7 0.0 copy-done.3
  22.7 0.0 copy-done.4
  22.7 0.0 copy-done.5
  22.7 0.0 copy-done.6
  22.7 0.0 copy-start.1
  22.7 1.7 %copy-done.1 = bf16[3,294912]{1,0:T(4,128)(2,1)S(1)} copy-done((bf16[3,294912]{1,0:T(4,128)(2,1)S(1)}, bf16[3,294912]{1,0:T(4,128)(2,1)}, u32[]{:S(2)}) %copy-start.1) | copy-done | bytes 1769496
  24.4 7.0 %resident_attention.1 = (bf16[1024,2,2,128]{3,2,1,0:T(2,128)(2,1)}, f32[1024,128]{1,0:T(8,128)S(1)}, bf16[256,576]{1,0:T(8,128)(2,1)S(1)}, bf16[128,576]{1,0:T(8,128)(2,1)S(1)}, f32[8,640]{1,0:T(8,128)S(1)}) custom-call(s32[3]{0:T(128)S(1)} %copy-done.6, s32[2,128]{1,0:T(2,128)S(1)} %copy-done.4, s32[2,128]{1,0:T(2,128)S(1)} %copy-done.5, ...), custom_call_target="tpu_custom_call" | custom-call | flops 1000000000 | bytes 8388608 | tf_op jit(solution)/shard_map/resident_attention/pallas_call | solution.py:208
  31.4 4.8 %all-to-all-done.blocks = bf16[128,9,2,128]{3,2,1,0:T(2,128)(2,1)S(1)} async-done(((bf16[128,9,2,128]{3,2,1,0:T(2,128)(2,1)}), bf16[128,9,2,128]{3,2,1,0:T(2,128)(2,1)S(1)}, u32[]{:S(2)}, u32[]{:S(2)}) %all-to-all-start) | async-done | bytes 589856 | tf_op jit(solution)/shard_map/all_to_all | solution.py:273
  36.3 0.7 %gather_blocks.1 = bf16[128,9,2,128]{3,2,1,0:T(2,128)(2,1)S(1)} custom-call(s32[128]{0:T(128)S(1)} %dynamic-slice_bitcast_fusion.sources, bf16[128,9,2,128]{3,2,1,0:T(2,128)(2,1)S(1)} %all-to-all-done.blocks), custom_call_target="tpu_custom_call" | custom-call | tf_op jit(solution)/shard_map/gather_blocks/pallas_call | solution.py:152
  37.0 25.0 %all_to_all.10 = bf16[128,9,2,128]{3,2,1,0:T(2,128)(2,1)S(1)} all-to-all(bf16[128,9,2,128]{3,2,1,0:T(2,128)(2,1)S(1)} %gather_blocks.1), channel_id=1, replica_groups={{127,126,125,124,123,122,121,120,119,118,117,116,115,114,113,112,111,11..., dimensions={0} | all-to-all | bytes 1179648 | tf_op jit(solution)/shard_map/all_to_all | solution.py:273
  62.0 2.1 %arrived_attention.1 = bf16[1024,2,2,128]{3,2,1,0:T(2,128)(2,1)} custom-call(f32[8,640]{1,0:T(8,128)S(1)} %get-tuple-element.12.penalties, bf16[256,576]{1,0:T(8,128)(2,1)S(1)} %get-tuple-element.13.queries, bf16[128,576]{1,0:T(8,128)(2,1)S(1)} %get-tuple-element.14.latents, bf16[2304,128]{1,0:T(8,128)(2,1)S(1)} %bitcast.7, ...), custom_call_target="tpu_custom_call", output_to_operand_aliasing={{}: (5, {})} | custom-call | tf_op jit(solution)/shard_map/arrived_attention/pallas_call | solution.py:255
  (1 shorter events, 0.0 us)
Async XLA Ops:
  0.0 1.3 %copy-start = (bf16[1,294912]{1,0:T(2,128)(2,1)S(1)}, bf16[1,294912]{1,0:T(2,128)(2,1)}, u32[]{:S(2)}) copy-start(bf16[1,294912]{1,0:T(2,128)(2,1)} %src.1) | copy-start | bytes 1769476
  1.5 21.1 %copy-start.2 = (bf16[4,147456]{1,0:T(4,128)(2,1)S(1)}, bf16[4,147456]{1,0:T(4,128)(2,1)}, u32[]{:S(2)}) copy-start(bf16[4,147456]{1,0:T(4,128)(2,1)} %queries.1) | copy-start | bytes 3538948
  1.6 21.1 %copy-start.3 = (bf16[4,1152]{1,0:T(4,128)(2,1)S(1)}, bf16[4,1152]{1,0:T(4,128)(2,1)}, u32[]{:S(2)}) copy-start(bf16[4,1152]{1,0:T(4,128)(2,1)} %new.1) | copy-start | bytes 27652
  1.6 21.1 %copy-start.4 = (s32[2,128]{1,0:T(2,128)S(1)}, s32[2,128]{1,0:T(2,128)}, u32[]{:S(2)}) copy-start(s32[2,128]{1,0:T(2,128)} %fresh_lengths.1) | copy-start | bytes 3076
  1.6 21.1 %copy-start.5 = (s32[2,128]{1,0:T(2,128)S(1)}, s32[2,128]{1,0:T(2,128)}, u32[]{:S(2)}) copy-start(s32[2,128]{1,0:T(2,128)} %matching.1) | copy-start | bytes 3076
  1.6 21.1 %copy-start.6 = (s32[3]{0:T(128)S(1)}, s32[3]{0:T(128)}, u32[]{:S(2)}) copy-start(s32[3]{0:T(128)} %lengths.1) | copy-start | bytes 40
  1.6 2.2 %collective-permute-start = (bf16[2304,128]{1,0:T(8,128)(2,1)S(1)}, bf16[2304,128]{1,0:T(8,128)(2,1)}, u32[]{:S(2)}, u32[]{:S(2)}) collective-permute-start(bf16[2304,128]{1,0:T(8,128)(2,1)S(1)} %fresh_rows.1), channel_id=1, source_target_pairs={{0,128},{128,0},{1,129},{129,1},{2,130},{130,2},{3,131},{131,3},{4... | collective-permute-start | bytes 1769480 | tf_op jit(solution)/shard_map/ppermute | solution.py:280
  5.9 30.4 %all-to-all-start = ((bf16[128,9,2,128]{3,2,1,0:T(2,128)(2,1)}), bf16[128,9,2,128]{3,2,1,0:T(2,128)(2,1)S(1)}, u32[]{:S(2)}, u32[]{:S(2)}) async-start(bf16[128,9,2,128]{3,2,1,0:T(2,128)(2,1)} %bitcast.1), calls=%async_computation | async-start | bytes 1179648 | tf_op jit(solution)/shard_map/all_to_all | solution.py:273
  22.7 1.7 %copy-start.1 = (bf16[3,294912]{1,0:T(4,128)(2,1)S(1)}, bf16[3,294912]{1,0:T(4,128)(2,1)}, u32[]{:S(2)}) copy-start(bf16[3,294912]{1,0:T(4,128)(2,1)} %caches.1) | copy-start | bytes 5308420

commit v6 on v5

--- a/solution.py
+++ b/solution.py
@@ -244,7 +244,7 @@
         place = pl.ds(step * size, size)
         pair_rows(both, rows, place)
         copy = pltpu.make_async_copy(rows.at[place], out.at[place, 1], sems.at[step])
-        copy.start()
+        copy.start(priority=step)
         copies.append(copy)
     for copy in copies:
         copy.wait()

time: 64.8 us -> 64.8 us (level)
  no operation moved by 1% of the time
where the time goes in v6:
time: 64.8 us; the launch traced here: 64.1 us
  blocking collectives  25 us (39%)
  starting transfers between devices  16.9 us (26%)
  Pallas kernels  12.1 us (19%)
  waiting for transfers between devices  6.96 us (11%)
  local copies, waits for them, and re-layouts  2.97 us (5%)
    all_to_all x1, blocking collectives, exchange(): lax.all_to_all(blocks, 'ep', split_axis=0, concat_axis=0, tiled=True, axi...  25 us
    all_to_all x1, starting transfers between devices, exchange(): lax.all_to_all(blocks, 'ep', split_axis=0, concat_axis=0, tiled=True, axi...  16.8 us
    pallas_call x1, Pallas kernels, resident_attention(): pl.pallas_call(resident_kernel, out_shape=(jax.ShapeDtypeStruct((CHUNKS,...  7.01 us
    all_to_all x1, waiting for transfers between devices, exchange(): lax.all_to_all(blocks, 'ep', split_axis=0, concat_axis=0, tiled=True, axi...  4.83 us
    unnamed x14, local copies, waits for them, and re-layouts  2.96 us
    ppermute x1, waiting for transfers between devices, per_device(): lax.ppermute(fresh_rows(fresh_cache), 'pool', [(0, 1), (1, 0)])  2.12 us
    pallas_call x1, Pallas kernels, arrived_attention(): pl.pallas_call(arrived_kernel, out_shape=jax.ShapeDtypeStruct(before.shap...  2.08 us
    pallas_call x1, Pallas kernels, taken_tiles(): pl.pallas_call(taken_kernel, out_shape=jax.ShapeDtypeStruct(rows.shape, B...  2.03 us
  transfers between devices with their start and end apart: 2, of which 2 were waited for; matrix products, arithmetic and copies ran while one was open for 0% of the time, Pallas kernels for 11%

profile of v6, /device:TPU:32, one launch (start us, length us, event | category | flops | bytes accessed | tf_op | source)
XLA Modules:
  0.0 64.1 jit_solution(10266147744709458871)
XLA Ops:
  0.0 0.0 copy-start
  0.0 1.3 %copy-done = bf16[1,294912]{1,0:T(2,128)(2,1)S(1)} copy-done((bf16[1,294912]{1,0:T(2,128)(2,1)S(1)}, bf16[1,294912]{1,0:T(2,128)(2,1)}, u32[]{:S(2)}) %copy-start) | copy-done | bytes 589848
  1.3 0.3 fresh_rows.1
  1.5 0.0 copy-start.2
  1.6 0.0 copy-start.3
  1.6 0.0 copy-start.4
  1.6 0.0 copy-start.5
  1.6 0.0 copy-start.6
  1.6 0.1 collective-permute-start
  1.7 2.1 %collective-permute-done.rows = bf16[2304,128]{1,0:T(8,128)(2,1)} collective-permute-done((bf16[2304,128]{1,0:T(8,128)(2,1)S(1)}, bf16[2304,128]{1,0:T(8,128)(2,1)}, u32[]{:S(2)}, u32[]{:S(2)}) %collective-permute-start) | collective-permute-done | bytes 589856 | tf_op jit(solution)/shard_map/ppermute | solution.py:280
  3.8 2.0 %taken_tiles.1 = bf16[2304,128]{1,0:T(8,128)(2,1)} custom-call(bf16[2304,128]{1,0:T(8,128)(2,1)} %collective-permute-done.rows), custom_call_target="tpu_custom_call", output_to_operand_aliasing={{}: (0, {})} | custom-call | tf_op jit(solution)/shard_map/taken_tiles/pallas_call | solution.py:128
  5.9 16.8 %all-to-all-start = ((bf16[128,9,2,128]{3,2,1,0:T(2,128)(2,1)}), bf16[128,9,2,128]{3,2,1,0:T(2,128)(2,1)S(1)}, u32[]{:S(2)}, u32[]{:S(2)}) async-start(bf16[128,9,2,128]{3,2,1,0:T(2,128)(2,1)} %bitcast.1), calls=%async_computation | async-start | bytes 1179648 | tf_op jit(solution)/shard_map/all_to_all | solution.py:273
  22.7 0.0 copy-done.2
  22.7 0.0 copy-done.3
  22.7 0.0 copy-done.4
  22.7 0.0 copy-done.5
  22.7 0.0 copy-done.6
  22.7 0.0 copy-start.1
  22.7 1.7 %copy-done.1 = bf16[3,294912]{1,0:T(4,128)(2,1)S(1)} copy-done((bf16[3,294912]{1,0:T(4,128)(2,1)S(1)}, bf16[3,294912]{1,0:T(4,128)(2,1)}, u32[]{:S(2)}) %copy-start.1) | copy-done | bytes 1769496
  24.4 7.0 %resident_attention.1 = (bf16[1024,2,2,128]{3,2,1,0:T(2,128)(2,1)}, f32[1024,128]{1,0:T(8,128)S(1)}, bf16[256,576]{1,0:T(8,128)(2,1)S(1)}, bf16[128,576]{1,0:T(8,128)(2,1)S(1)}, f32[8,640]{1,0:T(8,128)S(1)}) custom-call(s32[3]{0:T(128)S(1)} %copy-done.6, s32[2,128]{1,0:T(2,128)S(1)} %copy-done.4, s32[2,128]{1,0:T(2,128)S(1)} %copy-done.5, ...), custom_call_target="tpu_custom_call" | custom-call | flops 1000000000 | bytes 8388608 | tf_op jit(solution)/shard_map/resident_attention/pallas_call | solution.py:208
  31.4 4.8 %all-to-all-done.blocks = bf16[128,9,2,128]{3,2,1,0:T(2,128)(2,1)S(1)} async-done(((bf16[128,9,2,128]{3,2,1,0:T(2,128)(2,1)}), bf16[128,9,2,128]{3,2,1,0:T(2,128)(2,1)S(1)}, u32[]{:S(2)}, u32[]{:S(2)}) %all-to-all-start) | async-done | bytes 589856 | tf_op jit(solution)/shard_map/all_to_all | solution.py:273
  36.3 0.7 %gather_blocks.1 = bf16[128,9,2,128]{3,2,1,0:T(2,128)(2,1)S(1)} custom-call(s32[128]{0:T(128)S(1)} %dynamic-slice_bitcast_fusion.sources, bf16[128,9,2,128]{3,2,1,0:T(2,128)(2,1)S(1)} %all-to-all-done.blocks), custom_call_target="tpu_custom_call" | custom-call | tf_op jit(solution)/shard_map/gather_blocks/pallas_call | solution.py:152
  37.0 25.0 %all_to_all.10 = bf16[128,9,2,128]{3,2,1,0:T(2,128)(2,1)S(1)} all-to-all(bf16[128,9,2,128]{3,2,1,0:T(2,128)(2,1)S(1)} %gather_blocks.1), channel_id=1, replica_groups={{127,126,125,124,123,122,121,120,119,118,117,116,115,114,113,112,111,11..., dimensions={0} | all-to-all | bytes 1179648 | tf_op jit(solution)/shard_map/all_to_all | solution.py:273
  62.0 2.1 %arrived_attention.1 = bf16[1024,2,2,128]{3,2,1,0:T(2,128)(2,1)} custom-call(f32[8,640]{1,0:T(8,128)S(1)} %get-tuple-element.12.penalties, bf16[256,576]{1,0:T(8,128)(2,1)S(1)} %get-tuple-element.13.queries, bf16[128,576]{1,0:T(8,128)(2,1)S(1)} %get-tuple-element.14.latents, bf16[2304,128]{1,0:T(8,128)(2,1)S(1)} %bitcast.7, ...), custom_call_target="tpu_custom_call", output_to_operand_aliasing={{}: (5, {})} | custom-call | tf_op jit(solution)/shard_map/arrived_attention/pallas_call | solution.py:255
  (1 shorter events, 0.0 us)
Async XLA Ops:
  0.0 1.3 %copy-start = (bf16[1,294912]{1,0:T(2,128)(2,1)S(1)}, bf16[1,294912]{1,0:T(2,128)(2,1)}, u32[]{:S(2)}) copy-start(bf16[1,294912]{1,0:T(2,128)(2,1)} %src.1) | copy-start | bytes 1769476
  1.5 21.1 %copy-start.2 = (bf16[4,147456]{1,0:T(4,128)(2,1)S(1)}, bf16[4,147456]{1,0:T(4,128)(2,1)}, u32[]{:S(2)}) copy-start(bf16[4,147456]{1,0:T(4,128)(2,1)} %queries.1) | copy-start | bytes 3538948
  1.6 21.1 %copy-start.3 = (bf16[4,1152]{1,0:T(4,128)(2,1)S(1)}, bf16[4,1152]{1,0:T(4,128)(2,1)}, u32[]{:S(2)}) copy-start(bf16[4,1152]{1,0:T(4,128)(2,1)} %new.1) | copy-start | bytes 27652
  1.6 21.1 %copy-start.4 = (s32[2,128]{1,0:T(2,128)S(1)}, s32[2,128]{1,0:T(2,128)}, u32[]{:S(2)}) copy-start(s32[2,128]{1,0:T(2,128)} %fresh_lengths.1) | copy-start | bytes 3076
  1.6 21.1 %copy-start.5 = (s32[2,128]{1,0:T(2,128)S(1)}, s32[2,128]{1,0:T(2,128)}, u32[]{:S(2)}) copy-start(s32[2,128]{1,0:T(2,128)} %matching.1) | copy-start | bytes 3076
  1.6 21.1 %copy-start.6 = (s32[3]{0:T(128)S(1)}, s32[3]{0:T(128)}, u32[]{:S(2)}) copy-start(s32[3]{0:T(128)} %lengths.1) | copy-start | bytes 40
  1.6 2.2 %collective-permute-start = (bf16[2304,128]{1,0:T(8,128)(2,1)S(1)}, bf16[2304,128]{1,0:T(8,128)(2,1)}, u32[]{:S(2)}, u32[]{:S(2)}) collective-permute-start(bf16[2304,128]{1,0:T(8,128)(2,1)S(1)} %fresh_rows.1), channel_id=1, source_target_pairs={{0,128},{128,0},{1,129},{129,1},{2,130},{130,2},{3,131},{131,3},{4... | collective-permute-start | bytes 1769480 | tf_op jit(solution)/shard_map/ppermute | solution.py:280
  5.9 30.4 %all-to-all-start = ((bf16[128,9,2,128]{3,2,1,0:T(2,128)(2,1)}), bf16[128,9,2,128]{3,2,1,0:T(2,128)(2,1)S(1)}, u32[]{:S(2)}, u32[]{:S(2)}) async-start(bf16[128,9,2,128]{3,2,1,0:T(2,128)(2,1)} %bitcast.1), calls=%async_computation | async-start | bytes 1179648 | tf_op jit(solution)/shard_map/all_to_all | solution.py:273
  22.7 1.7 %copy-start.1 = (bf16[3,294912]{1,0:T(4,128)(2,1)S(1)}, bf16[3,294912]{1,0:T(4,128)(2,1)}, u32[]{:S(2)}) copy-start(bf16[3,294912]{1,0:T(4,128)(2,1)} %caches.1) | copy-start | bytes 5308420
